TPU v7x, 256 devices: a whole 4x4x8 slice. The times are simulated.
256 devices in a mesh: req: 8 (over z), head: 2 (over core), exp: 16 (over x, y).
Axes of the slice: x: 4, y: 4, z: 8, core: 2. Of those that a mesh axis runs over, the one named last changes fastest.
Arguments:
- queries: bfloat16 [32, 64, 32, 128], P('req', 'exp', 'head'), may hold values from -8 to 8
- new_keys: bfloat16 [32, 64, 4, 128], P('req', 'exp', 'head'), may hold values from -8 to 8
- new_values: bfloat16 [32, 64, 4, 128], P('req', 'exp', 'head'), may hold values from -6 to 6
- key_cache: bfloat16 [32, 24576, 4, 128], P('req', 'exp', 'head'), may hold values from -6 to 6
- value_cache: bfloat16 [32, 24576, 4, 128], P('req', 'exp', 'head'), may hold values from -6 to 6
- lengths: int32 [32], P('req'), may hold values from 1 to 24576, 262144 in all
- residual: bfloat16 [2048, 2048], P(('req', 'exp')), may hold values from -24 to 24
- out_weight: bfloat16 [4096, 2048], P('head', 'exp'), may hold values from -1.796875 to 1.796875
- norm_gain: float32 [2048], replicated, may hold values from 0.1 to 1.9
- route_ids: int32 [2048, 8], P(('req', 'exp')), may hold values from 0 to 127, all different within a row; in each aligned block of 16 rows (0 to 15, 16 to 31, ...) at most 2 rows name the same one
- route_weights: float32 [2048, 8], P(('req', 'exp')), may hold values from 0.05 to 0.3
- expert_in: bfloat16 [128, 2048, 2, 768], P(('req', 'exp'), None, None, 'head'), may hold values from -0.125 to 0.125
- expert_out: bfloat16 [128, 768, 2048], P(('req', 'exp'), 'head'), may hold values from -0.21875 to 0.21875
Outputs:
- output: bfloat16 [2048, 2048], P(('req', 'exp'), 'head')
Inputs may be any that keep to these rules, and one draw needn't show every extreme that they name: `route_ids`: each row names 8 different experts. Among the 16 rows of one device (aligned blocks of rows 0 to 15, 16 to 31 and so on) no expert is named by more than 2 rows.
All inputs are finite; a program needn't handle non-finite values. No bound on the sum of `lengths` on one device may be relied on, other than what follows from the above.
Results may differ from a plain program's by a relative error of at most 0.0051.
Values may be sent and summed in bfloat16 or wider, within the bound.
A program may use at most 128 MiB of HBM per device.

v0:
```python
import jax
import jax.numpy as jnp
from jax import lax
from jax.sharding import PartitionSpec as P

masked_score = -1e30
norm_epsilon = 1e-06


def normalize(value_sums, row_totals, heads_local):
    lead = value_sums.shape[:2]
    shaped = value_sums.reshape(lead[0], lead[1], heads_local, -1) / row_totals[..., None]
    return shaped.reshape(lead[0], lead[1], -1).astype(jnp.bfloat16)


def local(
    queries,
    new_keys,
    new_values,
    key_cache,
    value_cache,
    lengths,
    residual,
    out_weight,
    norm_gain,
    route_ids,
    route_weights,
    expert_in,
    expert_out,
):
    req_count, cache_span, kv_local, head_size = key_cache.shape
    heads_local = queries.shape[2]
    group_size = heads_local // kv_local
    score_scale = head_size ** (-0.5)
    whole_queries = lax.all_gather(queries, "exp", axis=1, tiled=True)
    block_rows = whole_queries.shape[1]
    grouped = whole_queries.reshape(req_count, block_rows, kv_local, group_size, head_size)
    cache_scores = (
        jnp.einsum("rbkgd,rskd->rkgbs", grouped, key_cache, preferred_element_type=jnp.float32)
        * score_scale
    )
    fresh_scores = (
        jnp.einsum("rbkgd,rnkd->rkgbn", grouped, new_keys, preferred_element_type=jnp.float32)
        * score_scale
    )
    positions = lax.axis_index("exp") * cache_span + lax.iota(jnp.int32, cache_span)
    valid_cache = positions[None, :] < lengths[:, None]
    cache_scores = jnp.where(valid_cache[:, None, None, None, :], cache_scores, masked_score)
    local_max = jnp.maximum(jnp.max(cache_scores, axis=-1), jnp.max(fresh_scores, axis=-1))
    row_max = lax.pmax(local_max, "exp")
    cache_exp = jnp.exp(cache_scores - row_max[..., None])
    fresh_exp = jnp.exp(fresh_scores - row_max[..., None])
    totals = jnp.sum(cache_exp, axis=-1) + jnp.sum(fresh_exp, axis=-1)
    weighted = jnp.einsum(
        "rkgbs,rskd->rbkgd",
        cache_exp.astype(jnp.bfloat16),
        value_cache,
        preferred_element_type=jnp.float32,
    )
    weighted = weighted + jnp.einsum(
        "rkgbn,rnkd->rbkgd",
        fresh_exp.astype(jnp.bfloat16),
        new_values,
        preferred_element_type=jnp.float32,
    )
    weighted = weighted.reshape(req_count, block_rows, heads_local * head_size)
    totals = jnp.transpose(totals, (0, 3, 1, 2)).reshape(req_count, block_rows, heads_local)
    all_sums, all_totals = lax.psum((weighted, totals), "exp")
    merged = normalize(all_sums, all_totals, heads_local)
    projected = jnp.dot(
        merged.reshape(req_count * block_rows, -1), out_weight, preferred_element_type=jnp.float32
    )
    projected = projected.reshape(req_count, block_rows, -1)
    projected = lax.psum(projected, "head")
    projected = projected.reshape(req_count * block_rows, projected.shape[-1])
    attn_out = lax.all_to_all(projected, "exp", split_axis=0, concat_axis=1, tiled=True)
    hidden = residual.astype(jnp.float32) + attn_out
    normed = (
        hidden
        * lax.rsqrt(jnp.mean(hidden * hidden, axis=-1, keepdims=True) + norm_epsilon)
        * norm_gain
    ).astype(jnp.bfloat16)
    row_count, model_width = normed.shape
    top_count = route_ids.shape[1]
    local_experts = expert_in.shape[0]
    groups = lax.axis_size("req") * lax.axis_size("exp")
    experts_all = local_experts * groups
    capacity = max(2, 2 * row_count * top_count // experts_all)
    expert_iota = lax.iota(jnp.int32, experts_all)
    named_count = jnp.sum((route_ids[:, :, None] == expert_iota).astype(jnp.int32), axis=1)
    earlier = jnp.cumsum(named_count, axis=0) - named_count
    slot_rank = jnp.take_along_axis(earlier, route_ids, axis=1)
    slot_index = route_ids * capacity + slot_rank
    slot_iota = lax.iota(jnp.int32, experts_all * capacity)
    placing = jnp.any(slot_index[None, :, :] == slot_iota[:, None, None], axis=2).astype(
        jnp.bfloat16
    )
    outgoing = jnp.dot(placing, normed, preferred_element_type=jnp.float32).astype(jnp.bfloat16)
    outgoing = outgoing.reshape(groups, local_experts, capacity, model_width)
    input_maps = expert_in.reshape(local_experts, model_width, -1)
    gate_up = jnp.einsum(
        "geci,eif->gecf",
        lax.all_to_all(outgoing, ("req", "exp"), split_axis=0, concat_axis=0, tiled=True),
        input_maps,
        preferred_element_type=jnp.float32,
    )
    half_units = gate_up.shape[-1] // 2
    activated = (jax.nn.silu(gate_up[..., :half_units]) * gate_up[..., half_units:]).astype(
        jnp.bfloat16
    )
    partial_value = jnp.einsum(
        "gecf,efi->geci", activated, expert_out, preferred_element_type=jnp.float32
    )
    half_width = model_width // lax.axis_size("head")
    head_start = lax.axis_index("head") * half_width
    returned_parts = lax.all_to_all(
        partial_value, ("req", "exp"), split_axis=0, concat_axis=0, tiled=True
    )
    both_halves = lax.psum(returned_parts, "head")
    returned = lax.dynamic_slice_in_dim(both_halves, head_start, half_width, 3).astype(jnp.bfloat16)
    flat_results = returned.reshape(experts_all * capacity, half_width)
    picked = jnp.take(flat_results, slot_index, axis=0).astype(jnp.float32)
    mixture = jnp.sum(picked * route_weights[:, :, None], axis=1)
    kept_hidden = lax.dynamic_slice_in_dim(hidden, head_start, half_width, 1)
    return (kept_hidden + mixture).astype(jnp.bfloat16)


def solution(mesh):
    return jax.shard_map(
        local,
        mesh=mesh,
        in_specs=(
            P("req", "exp", "head", None),
            P("req", "exp", "head", None),
            P("req", "exp", "head", None),
            P("req", "exp", "head", None),
            P("req", "exp", "head", None),
            P("req"),
            P(("req", "exp"), None),
            P("head", "exp"),
            P(),
            P(("req", "exp"), None),
            P(("req", "exp"), None),
            P(("req", "exp"), None, None, "head"),
            P(("req", "exp"), "head", None),
        ),
        out_specs=P(("req", "exp"), "head"),
        check_vma=False,
    )
```

profile of v0, /device:TPU:1, one launch (start us, length us, event | category | flops | bytes accessed | tf_op | source)
XLA Modules:
  0.0 439.8 jit_solution(7358443876455354545)
XLA Ops:
  9.0 51.0 %all-gather.2.cloned.1.call-done = bf16[4,64,16,128]{3,2,1,0:T(8,128)(2,1)} async-done(((bf16[4,4,16,128]{3,2,1,0:T(8,128)(2,1)}), bf16[4,64,16,128]{3,2,1,0:T(8,128)(2,1)}) %all-gather.2.cloned.1.call-update) | async-done | bytes 1048592 | tf_op jit(solution)/shard_map/all_gather | solution.py:35
  63.3 10.3 %bitcast_reduce_fusion = (f32[4,2,8,64]{3,2,1,0:T(8,128)S(1)}, f32[4,2,1536,64,8]{2,3,4,1,0:T(8,128)}) fusion(pred[4,1536]{1,0:T(4,128)(4,1)S(1)} %broadcast_compare_fusion, bf16[4,64,2,8,128]{4,1,3,2,0:T(8,128)(2,1)S(1)} %bitcast.75, bf16[4,1536,2,128,1]{3,2,1,0,4:T(2,128)(2,1)S(1)} %bitcast.76), kind=kOutput, calls=%fused_computation.3 | convolution fusion | flops 1629483008 | bytes 29382656 | tf_op jit(solution)/shard_map/rbkgd,rskd->rkgbs/dot_general | solution.py:39
  73.5 58.3 %pmax.7 = f32[4,2,8,64]{3,2,1,0:T(8,128)S(1)} all-reduce(f32[4,2,8,64]{3,2,1,0:T(8,128)S(1)} %max.5), channel_id=1, replica_groups=mesh['req'=8,'head'=2,'exp'=16] {'exp'}, use_global_device_ids=true, to_apply=%region_2.3 | all-reduce | flops 4096 | bytes 32768 | tf_op jit(solution)/shard_map/pmax | solution.py:50
  131.8 10.8 %fusion.3 = f32[4,2,8,64,128]{4,3,2,1,0:T(8,128)S(1)} fusion(f32[4,2,1536,64,8]{2,3,4,1,0:T(8,128)} %get-tuple-element.10, f32[4,2,8,64]{3,2,1,0:T(8,128)S(1)} %pmax.7, pred[4,1536]{1,0:T(4,128)(4,1)S(1)} %broadcast_compare_fusion, bf16[4,1536,2,128,1]{3,2,1,0,4:T(2,128)(2,1)S(1)} %bitcast.73), kind=kOutput, calls=%fused_computation.8 | convolution fusion | flops 1635778560 | bytes 30431232 | tf_op jit(solution)/shard_map/rkgbs,rskd->rbkgd/dot_general | solution.py:54
  143.2 2.6 copy.68
  145.8 2.7 reshape.99
  148.8 11.6 %fusion.1 = f32[4,2,8,64]{3,2,1,0:T(8,128)S(1)} fusion(f32[4,2,1536,64,8]{2,3,4,1,0:T(8,128)} %get-tuple-element.10, f32[4,2,8,64]{3,2,1,0:T(8,128)S(1)} %pmax.7, pred[4,1536]{1,0:T(4,128)(4,1)S(1)} %broadcast_compare_fusion), kind=kLoop, calls=%fused_computation.6 | loop fusion | flops 25161728 | bytes 25204736 | tf_op jit(solution)/shard_map/reduce_sum | solution.py:53
  160.5 55.6 %psum.29 = f32[4,64,16]{1,2,0:T(8,128)S(1)} all-reduce(f32[4,64,16]{1,2,0:T(8,128)S(1)} %add_bitcast_fusion.1), channel_id=1, replica_groups=mesh['req'=8,'head'=2,'exp'=16] {'exp'}, use_global_device_ids=true, to_apply=%region_6.7 | all-reduce | flops 4096 | bytes 32768 | tf_op jit(solution)/shard_map/psum | solution.py:68
  218.4 41.2 %all-reduce.4.cloned.1.call-done = f32[4,64,2048]{2,1,0:T(8,128)} async-done(((f32[4,64,2048]{2,1,0:T(8,128)}), f32[4,64,2048]{2,1,0:T(8,128)}) %all-reduce.4.cloned.1.call-update) | async-done | bytes 2097168 | tf_op jit(solution)/shard_map/psum | solution.py:68
  259.6 3.3 fusion.13
  264.6 28.5 %all-reduce.6.cloned.1.call-done = f32[16,16,128]{2,1,0:T(8,128)} async-done(((f32[16,16,128]{2,1,0:T(8,128)}), f32[16,16,128]{2,1,0:T(8,128)}) %all-reduce.6.cloned.1.call-update) | async-done | bytes 131088 | tf_op jit(solution)/shard_map/psum | solution.py:74
  293.1 6.3 %all-to-all-start = ((f32[16,16,128]{2,1,0:T(8,128)}), f32[16,16,128]{2,1,0:T(8,128)S(1)}, u32[]{:S(2)}, u32[]{:S(2)}) async-start(f32[16,16,128]{2,1,0:T(8,128)} %all-reduce.6.cloned.1.call-done), calls=%async_computation | async-start | bytes 262144 | tf_op jit(solution)/shard_map/all_to_all | solution.py:76
  299.6 6.5 %all-to-all-done = f32[16,16,128]{2,1,0:T(8,128)S(1)} async-done(((f32[16,16,128]{2,1,0:T(8,128)}), f32[16,16,128]{2,1,0:T(8,128)S(1)}, u32[]{:S(2)}, u32[]{:S(2)}) %all-to-all-start) | async-done | bytes 131104 | tf_op jit(solution)/shard_map/all_to_all | solution.py:76
  308.2 11.4 %all-to-all-start.1 = ((bf16[128,1,2,2048]{3,2,1,0:T(2,128)(2,1)}), bf16[128,1,2,2048]{3,2,1,0:T(2,128)(2,1)}, u32[]{:S(2)}, u32[]{:S(2)}) async-start(bf16[128,1,2,2048]{3,2,1,0:T(2,128)(2,1)} %bitcast.14), calls=%async_computation.1 | async-start | bytes 2097152 | tf_op jit(solution)/shard_map/all_to_all | solution.py:103
  319.7 6.8 %reshape.134 = bf16[2048,768,1]{1,0,2:T(8,128)(2,1)S(1)} reshape(bf16[1,2048,2,384]{3,2,1,0:T(2,128)(2,1)} %param.24) | data formatting | bytes 6291456 | tf_op jit(solution)/shard_map/reshape.3
  326.5 20.6 %all-to-all-done.1 = bf16[128,1,2,2048]{3,2,1,0:T(2,128)(2,1)} async-done(((bf16[128,1,2,2048]{3,2,1,0:T(2,128)(2,1)}), bf16[128,1,2,2048]{3,2,1,0:T(2,128)(2,1)}, u32[]{:S(2)}, u32[]{:S(2)}) %all-to-all-start.1) | async-done | bytes 1048608 | tf_op jit(solution)/shard_map/all_to_all | solution.py:103
  347.1 2.7 convolution_bitcast_fusion.1
  350.6 2.9 copy.78
  353.5 9.2 %all-to-all-start.2 = ((f32[128,1,2,2048]{3,2,1,0:T(2,128)}), f32[128,1,2,2048]{3,2,1,0:T(2,128)}, u32[]{:S(2)}, u32[]{:S(2)}) async-start(f32[128,1,2,2048]{3,2,1,0:T(2,128)} %copy.78), calls=%async_computation.2 | async-start | bytes 4194304 | tf_op jit(solution)/shard_map/all_to_all | solution.py:116
  363.1 47.1 %all-to-all-done.2 = f32[128,1,2,2048]{3,2,1,0:T(2,128)} async-done(((f32[128,1,2,2048]{3,2,1,0:T(2,128)}), f32[128,1,2,2048]{3,2,1,0:T(2,128)}, u32[]{:S(2)}, u32[]{:S(2)}) %all-to-all-start.2) | async-done | bytes 2097184 | tf_op jit(solution)/shard_map/all_to_all | solution.py:116
  410.2 15.8 %all-reduce.7 = bf16[128,1,2,2048]{3,2,1,0:T(2,128)(2,1)} all-reduce(f32[128,1,2,2048]{3,2,1,0:T(2,128)} %all-to-all-done.2), channel_id=1, replica_groups=mesh['req'=8,'head'=2,'exp'=16] {'head'}, use_global_device_ids=true, to_apply=%region_12.13 | all-reduce | flops 524288 | bytes 3145728 | tf_op jit(solution)/shard_map/psum | solution.py:119
  426.0 2.2 dynamic-slice_convert_fusion
  428.2 2.1 reshape.107
  430.2 2.2 gather_fusion
  (63 shorter events, 14.7 us)
Async XLA Ops:
  6.5 125.3 %copy-start = (bf16[4,1536,2,128]{3,2,1,0:T(2,128)(2,1)S(1)}, bf16[4,1536,2,128]{3,2,1,0:T(2,128)(2,1)}, u32[]{:S(2)}) copy-start(bf16[4,1536,2,128]{3,2,1,0:T(2,128)(2,1)} %param.17) | copy-start | bytes 9437188
  6.5 53.4 %all-gather.2.cloned.1.call-start = ((), (), s32[]{:S(2)}) async-start(), calls=%async_computation.3 | async-start | bytes 1114112 | tf_op jit(solution)/shard_map/all_gather | solution.py:35
  7.3 252.3 %all-reduce.4.cloned.1.call-start = ((), (), s32[]{:S(2)}) async-start(), calls=%async_computation.4 | async-start | bytes 4194304 | tf_op jit(solution)/shard_map/psum | solution.py:68
  60.0 3.3 copy-start.2
  131.8 10.8 %copy-start.6 = (bf16[4,4,2,128]{3,2,1,0:T(2,128)(2,1)S(1)}, bf16[4,4,2,128]{3,2,1,0:T(2,128)(2,1)}, u32[]{:S(2)}) copy-start(bf16[4,4,2,128]{3,2,1,0:T(2,128)(2,1)} %param.15) | copy-start | bytes 24580
  148.5 144.6 %all-reduce.6.cloned.1.call-start = ((), (), s32[]{:S(2)}) async-start(), calls=%async_computation.5 | async-start | bytes 262144 | tf_op jit(solution)/shard_map/psum | solution.py:74
  216.2 43.4 %copy-start.9 = (bf16[2048,128]{1,0:T(8,128)(2,1)S(1)}, bf16[2048,128]{1,0:T(8,128)(2,1)}, u32[]{:S(2)}) copy-start(bf16[2048,128]{1,0:T(8,128)(2,1)} %param.20) | copy-start | bytes 1572868
  218.4 44.6 %copy-start.5 = (s32[16,8]{0,1:T(8,128)S(1)}, s32[16,8]{0,1:T(8,128)}, u32[]{:S(2)}) copy-start(s32[16,8]{0,1:T(8,128)} %param.22) | copy-start | bytes 1540
  263.1 42.9 %copy-start.4 = (bf16[16,2048]{1,0:T(8,128)(2,1)S(1)}, bf16[16,2048]{1,0:T(8,128)(2,1)}, u32[]{:S(2)}) copy-start(bf16[16,2048]{1,0:T(8,128)(2,1)} %param.19) | copy-start | bytes 196612
  263.1 43.1 %copy-start.7 = (f32[2048]{0:T(1024)S(1)}, f32[2048]{0:T(1024)}, u32[]{:S(2)}) copy-start(f32[2048]{0:T(1024)} %param.21) | copy-start | bytes 24580
  293.1 13.0 %all-to-all-start = ((f32[16,16,128]{2,1,0:T(8,128)}), f32[16,16,128]{2,1,0:T(8,128)S(1)}, u32[]{:S(2)}, u32[]{:S(2)}) async-start(f32[16,16,128]{2,1,0:T(8,128)} %all-reduce.6.cloned.1.call-done), calls=%async_computation | async-start | bytes 262144 | tf_op jit(solution)/shard_map/all_to_all | solution.py:76
  308.2 38.9 %all-to-all-start.1 = ((bf16[128,1,2,2048]{3,2,1,0:T(2,128)(2,1)}), bf16[128,1,2,2048]{3,2,1,0:T(2,128)(2,1)}, u32[]{:S(2)}, u32[]{:S(2)}) async-start(bf16[128,1,2,2048]{3,2,1,0:T(2,128)(2,1)} %bitcast.14), calls=%async_computation.1 | async-start | bytes 2097152 | tf_op jit(solution)/shard_map/all_to_all | solution.py:103
  347.1 2.7 copy-start.3
  353.5 9.5 %copy-start.8 = (f32[16,8]{0,1:T(8,128)S(1)}, f32[16,8]{0,1:T(8,128)}, u32[]{:S(2)}) copy-start(f32[16,8]{0,1:T(8,128)} %param.23) | copy-start | bytes 1540
  353.5 56.7 %all-to-all-start.2 = ((f32[128,1,2,2048]{3,2,1,0:T(2,128)}), f32[128,1,2,2048]{3,2,1,0:T(2,128)}, u32[]{:S(2)}, u32[]{:S(2)}) async-start(f32[128,1,2,2048]{3,2,1,0:T(2,128)} %copy.78), calls=%async_computation.2 | async-start | bytes 4194304 | tf_op jit(solution)/shard_map/all_to_all | solution.py:116
  410.2 23.1 %copy-start.1 = (bf16[4,1536,2,128]{3,2,1,0:T(2,128)(2,1)S(1)}, bf16[4,1536,2,128]{3,2,1,0:T(2,128)(2,1)}, u32[]{:S(2)}) copy-start(bf16[4,1536,2,128]{3,2,1,0:T(2,128)(2,1)} %param.17) | copy-start | bytes 9437188
Sparse Core Ops, SparseCore 0:
  9.8 50.0 all-gather.1
  148.6 110.9 all-reduce.3
  263.1 29.9 all-reduce.5
where the time goes:
time: 441 us; the launch traced here: 440 us
  waiting for transfers between devices  196 us (44%)
  blocking collectives  130 us (29%)
  matrix products  30.5 us (7%)
  local copies, waits for them, and re-layouts  29.7 us (7%)
  starting transfers between devices  27 us (6%)
  other arithmetic  13.8 us (3%)
  between operations  13.4 us (3%)
    pmax x1, blocking collectives, local(): row_max = lax.pmax(local_max, 'exp')  58.3 us
    psum x1, blocking collectives, local(): all_sums, all_totals = lax.psum((weighted, totals), 'exp')  55.6 us
    all_gather x1, waiting for transfers between devices, local(): whole_queries = lax.all_gather(queries, 'exp', axis=1, tiled=True)  51 us
    all_to_all x1, waiting for transfers between devices, local(): lax.all_to_all(partial_value, ('req', 'exp'), split_axis=0, concat_axis=0...  47.1 us
    psum x1, waiting for transfers between devices, local(): all_sums, all_totals = lax.psum((weighted, totals), 'exp')  41.2 us
    psum x1, waiting for transfers between devices, local(): projected = lax.psum(projected, 'head')  28.5 us
    all_to_all x1, waiting for transfers between devices, local(): lax.all_to_all(outgoing, ('req', 'exp'), split_axis=0, concat_axis=0, til...  20.6 us
    psum x1, blocking collectives, local(): both_halves = lax.psum(returned_parts, 'head')  15.8 us
  transfers between devices with their start and end apart: 6, of which 6 were waited for; matrix products, arithmetic and copies ran while one was open for 6% of the time, Pallas kernels for 0%

commit v1 on v0

--- a/solution.py
+++ b/solution.py
@@ -88,7 +88,9 @@
     capacity = max(2, 2 * row_count * top_count // experts_all)
     expert_iota = lax.iota(jnp.int32, experts_all)
     named_count = jnp.sum((route_ids[:, :, None] == expert_iota).astype(jnp.int32), axis=1)
-    earlier = jnp.cumsum(named_count, axis=0) - named_count
+    row_iota = lax.iota(jnp.int32, row_count)
+    before = (row_iota[None, :] < row_iota[:, None]).astype(jnp.int32)
+    earlier = jnp.sum(before[:, :, None] * named_count[None], axis=1)
     slot_rank = jnp.take_along_axis(earlier, route_ids, axis=1)
     slot_index = route_ids * capacity + slot_rank
     slot_iota = lax.iota(jnp.int32, experts_all * capacity)

time: 441 us -> 441 us (level)
  no operation moved by 1% of the time
where the time goes in v1:
time: 441 us; the launch traced here: 440 us
  waiting for transfers between devices  195 us (44%)
  blocking collectives  130 us (29%)
  matrix products  30.5 us (7%)
  local copies, waits for them, and re-layouts  29.7 us (7%)
  starting transfers between devices  27 us (6%)
  other arithmetic  14.6 us (3%)
  between operations  13.4 us (3%)
    pmax x1, blocking collectives, local(): row_max = lax.pmax(local_max, 'exp')  58.3 us
    psum x1, blocking collectives, local(): all_sums, all_totals = lax.psum((weighted, totals), 'exp')  55.6 us
    all_gather x1, waiting for transfers between devices, local(): whole_queries = lax.all_gather(queries, 'exp', axis=1, tiled=True)  50.3 us
    all_to_all x1, waiting for transfers between devices, local(): lax.all_to_all(partial_value, ('req', 'exp'), split_axis=0, concat_axis=0...  47.1 us
    psum x1, waiting for transfers between devices, local(): all_sums, all_totals = lax.psum((weighted, totals), 'exp')  41.3 us
    psum x1, waiting for transfers between devices, local(): projected = lax.psum(projected, 'head')  28.4 us
    all_to_all x1, waiting for transfers between devices, local(): lax.all_to_all(outgoing, ('req', 'exp'), split_axis=0, concat_axis=0, til...  20.6 us
    psum x1, blocking collectives, local(): both_halves = lax.psum(returned_parts, 'head')  15.8 us
  transfers between devices with their start and end apart: 6, of which 6 were waited for; matrix products, arithmetic and copies ran while one was open for 6% of the time, Pallas kernels for 0%

profile of v1, /device:TPU:1, one launch (start us, length us, event | category | flops | bytes accessed | tf_op | source)
XLA Modules:
  0.0 439.8 jit_solution(11787802310517673241)
XLA Ops:
  9.7 50.3 %all-gather.2.cloned.1.call-done = bf16[4,64,16,128]{3,2,1,0:T(8,128)(2,1)} async-done(((bf16[4,4,16,128]{3,2,1,0:T(8,128)(2,1)}), bf16[4,64,16,128]{3,2,1,0:T(8,128)(2,1)}) %all-gather.2.cloned.1.call-update) | async-done | bytes 1048592 | tf_op jit(solution)/shard_map/all_gather | solution.py:35
  63.3 10.3 %bitcast_reduce_fusion = (f32[4,2,8,64]{3,2,1,0:T(8,128)S(1)}, f32[4,2,1536,64,8]{2,3,4,1,0:T(8,128)}) fusion(pred[4,1536]{1,0:T(4,128)(4,1)S(1)} %broadcast_compare_fusion, bf16[4,64,2,8,128]{4,1,3,2,0:T(8,128)(2,1)S(1)} %bitcast.75, bf16[4,1536,2,128,1]{3,2,1,0,4:T(2,128)(2,1)S(1)} %bitcast.76), kind=kOutput, calls=%fused_computation.3 | convolution fusion | flops 1629483008 | bytes 29382656 | tf_op jit(solution)/shard_map/rbkgd,rskd->rkgbs/dot_general | solution.py:39
  73.5 58.3 %pmax.7 = f32[4,2,8,64]{3,2,1,0:T(8,128)S(1)} all-reduce(f32[4,2,8,64]{3,2,1,0:T(8,128)S(1)} %max.5), channel_id=1, replica_groups=mesh['req'=8,'head'=2,'exp'=16] {'exp'}, use_global_device_ids=true, to_apply=%region_2.3 | all-reduce | flops 4096 | bytes 32768 | tf_op jit(solution)/shard_map/pmax | solution.py:50
  131.8 10.8 %fusion.3 = f32[4,2,8,64,128]{4,3,2,1,0:T(8,128)S(1)} fusion(f32[4,2,1536,64,8]{2,3,4,1,0:T(8,128)} %get-tuple-element.10, f32[4,2,8,64]{3,2,1,0:T(8,128)S(1)} %pmax.7, pred[4,1536]{1,0:T(4,128)(4,1)S(1)} %broadcast_compare_fusion, bf16[4,1536,2,128,1]{3,2,1,0,4:T(2,128)(2,1)S(1)} %bitcast.73), kind=kOutput, calls=%fused_computation.8 | convolution fusion | flops 1635778560 | bytes 30431232 | tf_op jit(solution)/shard_map/rkgbs,rskd->rbkgd/dot_general | solution.py:54
  143.2 2.6 copy.68
  145.8 2.7 reshape.113
  148.8 11.6 %fusion.1 = f32[4,2,8,64]{3,2,1,0:T(8,128)S(1)} fusion(f32[4,2,1536,64,8]{2,3,4,1,0:T(8,128)} %get-tuple-element.10, f32[4,2,8,64]{3,2,1,0:T(8,128)S(1)} %pmax.7, pred[4,1536]{1,0:T(4,128)(4,1)S(1)} %broadcast_compare_fusion), kind=kLoop, calls=%fused_computation.6 | loop fusion | flops 25161728 | bytes 25204736 | tf_op jit(solution)/shard_map/reduce_sum | solution.py:53
  160.4 55.6 %psum.29 = f32[4,64,16]{1,2,0:T(8,128)S(1)} all-reduce(f32[4,64,16]{1,2,0:T(8,128)S(1)} %add_bitcast_fusion.1), channel_id=1, replica_groups=mesh['req'=8,'head'=2,'exp'=16] {'exp'}, use_global_device_ids=true, to_apply=%region_6.7 | all-reduce | flops 4096 | bytes 32768 | tf_op jit(solution)/shard_map/psum | solution.py:68
  218.3 41.3 %all-reduce.4.cloned.1.call-done = f32[4,64,2048]{2,1,0:T(8,128)} async-done(((f32[4,64,2048]{2,1,0:T(8,128)}), f32[4,64,2048]{2,1,0:T(8,128)}) %all-reduce.4.cloned.1.call-update) | async-done | bytes 2097168 | tf_op jit(solution)/shard_map/psum | solution.py:68
  259.6 3.3 fusion.13
  264.7 28.4 %all-reduce.6.cloned.1.call-done = f32[16,16,128]{2,1,0:T(8,128)} async-done(((f32[16,16,128]{2,1,0:T(8,128)}), f32[16,16,128]{2,1,0:T(8,128)}) %all-reduce.6.cloned.1.call-update) | async-done | bytes 131088 | tf_op jit(solution)/shard_map/psum | solution.py:74
  293.1 6.3 %all-to-all-start = ((f32[16,16,128]{2,1,0:T(8,128)}), f32[16,16,128]{2,1,0:T(8,128)S(1)}, u32[]{:S(2)}, u32[]{:S(2)}) async-start(f32[16,16,128]{2,1,0:T(8,128)} %all-reduce.6.cloned.1.call-done), calls=%async_computation | async-start | bytes 262144 | tf_op jit(solution)/shard_map/all_to_all | solution.py:76
  299.6 6.5 %all-to-all-done = f32[16,16,128]{2,1,0:T(8,128)S(1)} async-done(((f32[16,16,128]{2,1,0:T(8,128)}), f32[16,16,128]{2,1,0:T(8,128)S(1)}, u32[]{:S(2)}, u32[]{:S(2)}) %all-to-all-start) | async-done | bytes 131104 | tf_op jit(solution)/shard_map/all_to_all | solution.py:76
  308.2 11.4 %all-to-all-start.1 = ((bf16[128,1,2,2048]{3,2,1,0:T(2,128)(2,1)}), bf16[128,1,2,2048]{3,2,1,0:T(2,128)(2,1)}, u32[]{:S(2)}, u32[]{:S(2)}) async-start(bf16[128,1,2,2048]{3,2,1,0:T(2,128)(2,1)} %bitcast.14), calls=%async_computation.1 | async-start | bytes 2097152 | tf_op jit(solution)/shard_map/all_to_all | solution.py:105
  319.6 6.8 %reshape.148 = bf16[2048,768,1]{1,0,2:T(8,128)(2,1)S(1)} reshape(bf16[1,2048,2,384]{3,2,1,0:T(2,128)(2,1)} %param.24) | data formatting | bytes 6291456 | tf_op jit(solution)/shard_map/reshape.3
  326.5 20.6 %all-to-all-done.1 = bf16[128,1,2,2048]{3,2,1,0:T(2,128)(2,1)} async-done(((bf16[128,1,2,2048]{3,2,1,0:T(2,128)(2,1)}), bf16[128,1,2,2048]{3,2,1,0:T(2,128)(2,1)}, u32[]{:S(2)}, u32[]{:S(2)}) %all-to-all-start.1) | async-done | bytes 1048608 | tf_op jit(solution)/shard_map/all_to_all | solution.py:105
  347.1 2.7 convolution_bitcast_fusion.1
  350.6 2.9 copy.78
  353.5 9.2 %all-to-all-start.2 = ((f32[128,1,2,2048]{3,2,1,0:T(2,128)}), f32[128,1,2,2048]{3,2,1,0:T(2,128)}, u32[]{:S(2)}, u32[]{:S(2)}) async-start(f32[128,1,2,2048]{3,2,1,0:T(2,128)} %copy.78), calls=%async_computation.2 | async-start | bytes 4194304 | tf_op jit(solution)/shard_map/all_to_all | solution.py:118
  363.0 47.1 %all-to-all-done.2 = f32[128,1,2,2048]{3,2,1,0:T(2,128)} async-done(((f32[128,1,2,2048]{3,2,1,0:T(2,128)}), f32[128,1,2,2048]{3,2,1,0:T(2,128)}, u32[]{:S(2)}, u32[]{:S(2)}) %all-to-all-start.2) | async-done | bytes 2097184 | tf_op jit(solution)/shard_map/all_to_all | solution.py:118
  410.2 15.8 %all-reduce.7 = bf16[128,1,2,2048]{3,2,1,0:T(2,128)(2,1)} all-reduce(f32[128,1,2,2048]{3,2,1,0:T(2,128)} %all-to-all-done.2), channel_id=1, replica_groups=mesh['req'=8,'head'=2,'exp'=16] {'head'}, use_global_device_ids=true, to_apply=%region_12.13 | all-reduce | flops 524288 | bytes 3145728 | tf_op jit(solution)/shard_map/psum | solution.py:121
  426.0 2.2 dynamic-slice_convert_fusion
  428.1 2.1 reshape.121
  430.2 2.2 gather_fusion
  (63 shorter events, 15.5 us)
Async XLA Ops:
  6.5 125.3 %copy-start = (bf16[4,1536,2,128]{3,2,1,0:T(2,128)(2,1)S(1)}, bf16[4,1536,2,128]{3,2,1,0:T(2,128)(2,1)}, u32[]{:S(2)}) copy-start(bf16[4,1536,2,128]{3,2,1,0:T(2,128)(2,1)} %param.17) | copy-start | bytes 9437188
  6.5 53.4 %all-gather.2.cloned.1.call-start = ((), (), s32[]{:S(2)}) async-start(), calls=%async_computation.3 | async-start | bytes 1114112 | tf_op jit(solution)/shard_map/all_gather | solution.py:35
  7.3 252.3 %all-reduce.4.cloned.1.call-start = ((), (), s32[]{:S(2)}) async-start(), calls=%async_computation.4 | async-start | bytes 4194304 | tf_op jit(solution)/shard_map/psum | solution.py:68
  60.0 3.3 copy-start.2
  131.8 10.8 %copy-start.6 = (bf16[4,4,2,128]{3,2,1,0:T(2,128)(2,1)S(1)}, bf16[4,4,2,128]{3,2,1,0:T(2,128)(2,1)}, u32[]{:S(2)}) copy-start(bf16[4,4,2,128]{3,2,1,0:T(2,128)(2,1)} %param.15) | copy-start | bytes 24580
  148.5 144.6 %all-reduce.6.cloned.1.call-start = ((), (), s32[]{:S(2)}) async-start(), calls=%async_computation.5 | async-start | bytes 262144 | tf_op jit(solution)/shard_map/psum | solution.py:74
  216.1 43.4 %copy-start.9 = (bf16[2048,128]{1,0:T(8,128)(2,1)S(1)}, bf16[2048,128]{1,0:T(8,128)(2,1)}, u32[]{:S(2)}) copy-start(bf16[2048,128]{1,0:T(8,128)(2,1)} %param.20) | copy-start | bytes 1572868
  263.2 36.1 %copy-start.5 = (s32[16,8]{0,1:T(8,128)S(1)}, s32[16,8]{0,1:T(8,128)}, u32[]{:S(2)}) copy-start(s32[16,8]{0,1:T(8,128)} %param.22) | copy-start | bytes 1540
  263.2 42.8 %copy-start.4 = (bf16[16,2048]{1,0:T(8,128)(2,1)S(1)}, bf16[16,2048]{1,0:T(8,128)(2,1)}, u32[]{:S(2)}) copy-start(bf16[16,2048]{1,0:T(8,128)(2,1)} %param.19) | copy-start | bytes 196612
  263.2 43.0 %copy-start.7 = (f32[2048]{0:T(1024)S(1)}, f32[2048]{0:T(1024)}, u32[]{:S(2)}) copy-start(f32[2048]{0:T(1024)} %param.21) | copy-start | bytes 24580
  293.1 13.0 %all-to-all-start = ((f32[16,16,128]{2,1,0:T(8,128)}), f32[16,16,128]{2,1,0:T(8,128)S(1)}, u32[]{:S(2)}, u32[]{:S(2)}) async-start(f32[16,16,128]{2,1,0:T(8,128)} %all-reduce.6.cloned.1.call-done), calls=%async_computation | async-start | bytes 262144 | tf_op jit(solution)/shard_map/all_to_all | solution.py:76
  308.2 38.9 %all-to-all-start.1 = ((bf16[128,1,2,2048]{3,2,1,0:T(2,128)(2,1)}), bf16[128,1,2,2048]{3,2,1,0:T(2,128)(2,1)}, u32[]{:S(2)}, u32[]{:S(2)}) async-start(bf16[128,1,2,2048]{3,2,1,0:T(2,128)(2,1)} %bitcast.14), calls=%async_computation.1 | async-start | bytes 2097152 | tf_op jit(solution)/shard_map/all_to_all | solution.py:105
  347.1 2.7 copy-start.3
  353.5 9.5 %copy-start.8 = (f32[16,8]{0,1:T(8,128)S(1)}, f32[16,8]{0,1:T(8,128)}, u32[]{:S(2)}) copy-start(f32[16,8]{0,1:T(8,128)} %param.23) | copy-start | bytes 1540
  353.5 56.7 %all-to-all-start.2 = ((f32[128,1,2,2048]{3,2,1,0:T(2,128)}), f32[128,1,2,2048]{3,2,1,0:T(2,128)}, u32[]{:S(2)}, u32[]{:S(2)}) async-start(f32[128,1,2,2048]{3,2,1,0:T(2,128)} %copy.78), calls=%async_computation.2 | async-start | bytes 4194304 | tf_op jit(solution)/shard_map/all_to_all | solution.py:118
  410.2 23.1 %copy-start.1 = (bf16[4,1536,2,128]{3,2,1,0:T(2,128)(2,1)S(1)}, bf16[4,1536,2,128]{3,2,1,0:T(2,128)(2,1)}, u32[]{:S(2)}) copy-start(bf16[4,1536,2,128]{3,2,1,0:T(2,128)(2,1)} %param.17) | copy-start | bytes 9437188
Sparse Core Ops, SparseCore 0:
  9.8 50.0 all-gather.1
  148.6 110.8 all-reduce.3
  263.0 29.9 all-reduce.5

commit v2 on v0

v2 whole, which is shorter than its diff:
```python
import functools
import math

import jax
import jax.numpy as jnp
from jax import lax
from jax.experimental import pallas as pl
from jax.experimental.pallas import tpu as pltpu
from jax.sharding import PartitionSpec as P

masked_score = -1e30
norm_epsilon = 1e-06
MESH = pl.DeviceIdType.MESH
BF = jnp.bfloat16
F32 = jnp.float32
PLANE = 16
DEPTH = 8
TILE = 256
TURN = 128
VMEM_LIMIT = 60 * 1024 * 1024


def place():
    return lax.axis_index("req"), lax.axis_index("head"), lax.axis_index("exp")


def remote(src, dst, send_sem, recv_sem, target):
    return pltpu.make_async_remote_copy(
        src_ref=src,
        dst_ref=dst,
        send_sem=send_sem,
        recv_sem=recv_sem,
        device_id=target,
        device_id_type=MESH,
    )


def rows16(index):
    return pl.ds(pl.multiple_of(index * 16, 16), 16)


def layer_kernel(
    span,
    q_ref,
    nk_ref,
    nv_ref,
    k_hbm,
    v_hbm,
    len_ref,
    res_ref,
    w_hbm,
    gain_ref,
    ids_ref,
    wts_ref,
    in_hbm,
    down_hbm,
    out_ref,
    raw,
    loose,
    k_ref,
    v_ref,
    bias,
    qbuf,
    scores_a,
    scores_b,
    probs_a,
    probs_b,
    stage,
    recv,
    split,
    flat,
    abuf,
    w_ref,
    pstage,
    pbuf,
    hid_ref,
    sq_stage,
    sq_recv,
    norm_ref,
    in_raw,
    in_ref,
    down_ref,
    meta_ref,
    zbuf,
    mbuf,
    xstage,
    xbuf,
    ystage,
    ybuf,
    rstage,
    rbuf,
    cstage,
    cbuf,
    kv_sems,
    w_sems,
    q_send,
    q_recv,
    f_send,
    f_recv,
    s_send,
    s_recv,
    a_send,
    a_recv,
    b_send,
    b_recv,
    p_send,
    p_recv,
    sq_sems,
    z_send,
    z_recv,
    m_send,
    m_recv,
    x_send,
    x_recv,
    h_send,
    h_recv,
    y_sems,
    r_send,
    r_recv,
    c_send,
    c_recv,
):
    z, c, me = place()
    other = 1 - c
    row_x = lax.div(me, 4)
    row_y = lax.rem(me, 4)

    def kv_copy(which, request):
        source = (k_hbm, v_hbm)[which]
        return pltpu.make_async_copy(
            source.at[request], raw.at[which, request], kv_sems.at[which, request]
        )

    def w_copy(which):
        source, target = ((w_hbm, w_ref), (in_hbm, in_raw), (down_hbm, down_ref))[which]
        return pltpu.make_async_copy(source, target, w_sems.at[which])

    @pl.loop(0, 4)
    def _(i):
        request = lax.rem(row_y + i, 4)
        kv_copy(0, request).start()
        kv_copy(1, request).start()

    for which in range(3):
        w_copy(which).start()

    barrier = pltpu.get_barrier_semaphore()

    def greet(*target):
        pl.semaphore_signal(barrier, inc=1, device_id=target, device_id_type=MESH)

    @pl.loop(1, PLANE)
    def _(i):
        peer = lax.rem(me + i, PLANE)
        greet(z, c, peer)
        greet(z, other, peer)

    @pl.loop(1, DEPTH)
    def _(i):
        greet(lax.rem(z + i, DEPTH), c, me)

    greet(z, other, me)
    meta_ref[...] = jnp.zeros((16, 128), F32)
    meta_ref[0:8, 0:16] = ids_ref[...].astype(F32)
    meta_ref[8:16, 0:16] = wts_ref[...]
    meta_ref[...] = pltpu.roll(meta_ref[...], 16 * z, 1)
    pl.semaphore_wait(barrier, 2 * PLANE - 1 + DEPTH - 1)

    def q_copy(source, target):
        return remote(
            q_ref,
            qbuf.at[:, pl.ds(pl.multiple_of((row_x * 4 + source) * 64, 64), 64), :],
            q_send.at[target],
            q_recv.at[source],
            (z, c, row_x * 4 + target),
        )

    @pl.loop(1, 4)
    def _(i):
        q_copy(row_y, lax.rem(row_y + i, 4)).start()

    def m_copy(source, target):
        return remote(
            meta_ref, mbuf.at[source], m_send.at[target], m_recv.at[source], (target, c, me)
        )

    @pl.loop(1, DEPTH)
    def _(i):
        m_copy(z, lax.rem(z + i, DEPTH)).start()

    mbuf[z] = meta_ref[...]
    qbuf[:, pl.ds(pl.multiple_of(me * 64, 64), 64), :] = q_ref[...]

    def f_copy(source, target):
        rows = pl.ds(pl.multiple_of(source * 256, 256), 256)
        return remote(
            qbuf.at[:, rows, :],
            qbuf.at[:, rows, :],
            f_send.at[target],
            f_recv.at[source],
            (z, c, target * 4 + row_y),
        )

    keys = span + 128
    key_iota = lax.broadcasted_iota(jnp.int32, (8, keys), 1)

    def arrange(request):
        cached = jnp.logical_and(key_iota < span, key_iota + me * span < len_ref[request])
        fresh = jnp.logical_and(key_iota >= span, key_iota < span + 4)
        bias[request] = jnp.where(jnp.logical_or(cached, fresh), 0.0, masked_score)
        for which in range(2):
            target = (k_ref, v_ref)[which]
            new = (nk_ref, nv_ref)[which]
            kv_copy(which, request).wait()

            @pl.loop(0, span // TILE)
            def _(i):
                rows = pl.ds(pl.multiple_of(i * 2 * TILE, 2 * TILE), 2 * TILE)
                loose[...] = raw[which, request, rows, :].astype(F32)
                into = pl.ds(pl.multiple_of(i * TILE, TILE), TILE)
                target[request, into, 0:128] = loose[pl.ds(0, TILE, 2), :].astype(BF)
                target[request, into, 128:256] = loose[pl.ds(1, TILE, 2), :].astype(BF)

            loose[0:8, :] = new[request].astype(F32)
            loose[8:256, :] = jnp.zeros((248, 128), F32)
            tail = pl.ds(span, 128)
            target[request, tail, 0:128] = loose[pl.ds(0, 128, 2), :].astype(BF)
            target[request, tail, 128:256] = loose[pl.ds(1, 128, 2), :].astype(BF)

    arrange(row_y)

    @pl.loop(1, 4)
    def _(i):
        q_copy(lax.rem(row_y + i, 4), row_y).wait_recv()

    f_copy(row_x, lax.rem(row_x + 3, 4)).start()
    f_copy(row_x, lax.rem(row_x + 1, 4)).start()

    row_iota = lax.broadcasted_iota(jnp.int32, (256, 128), 0)
    low = lax.rem(row_iota, 16) < 8
    low_mask = jnp.where(low, 1.0, 0.0).astype(BF)
    high_mask = jnp.where(low, 0.0, 1.0).astype(BF)
    stat_iota = lax.broadcasted_iota(jnp.int32, (16, 128), 0)
    factor = (128.0 ** -0.5) * math.log2(math.e)
    tiles = [slice(t * 128, t * 128 + 128) for t in range(keys // 128)]

    def s_copy(owner, source):
        return remote(
            stage.at[owner],
            recv.at[source],
            s_send.at[owner],
            s_recv.at[source],
            (z, c, owner),
        )

    def score(request, group, scores):
        q = qbuf[request, pl.ds(pl.multiple_of(group * 256, 256), 256), :]
        both = jnp.concatenate([q * low_mask, q * high_mask], axis=1)
        scores[...] = lax.dot_general(
            both, k_ref[request], (((1,), (1,)), ((), ())), preferred_element_type=F32
        )

    def soften(request, scores, probs):
        levels, totals = [], []
        for part in range(2):
            rows = slice(part * 128, part * 128 + 128)
            top = scores[rows, tiles[0]] + bias[request, 0:1, tiles[0]]
            for tile in tiles[1:]:
                top = jnp.maximum(top, scores[rows, tile] + bias[request, 0:1, tile])
            shift = jnp.max(top, axis=1, keepdims=True) * factor
            total = jnp.zeros((128, 128), F32)
            for tile in tiles:
                shown = scores[rows, tile] + bias[request, 0:1, tile]
                prob = jnp.exp2(shown * factor - shift)
                total = total + prob
                probs[rows, tile] = prob.astype(BF)
            total = jnp.sum(total, axis=1, keepdims=True)
            levels.append(shift + jnp.log2(total))
            totals.append(total)
        return jnp.concatenate(levels, axis=0), jnp.concatenate(totals, axis=0)

    def finish(owner, request, probs, level, total):
        sums = jnp.dot(probs[...], v_ref[request], preferred_element_type=F32)
        mean = jnp.where(low, sums[:, :128], sums[:, 128:]) / total
        turned = jnp.transpose(jnp.broadcast_to(level, (256, 128)))[0:1, :]
        stats = jnp.zeros((16, 128), F32)
        for half in range(2):
            rest = turned[:, half * 128 : half * 128 + 128]
            for term in range(3):
                part = rest.astype(BF).astype(F32)
                rest = rest - part
                stats = jnp.where(stat_iota == 2 * term + half, part, stats)
        stage[owner, 0:256, :] = mean.astype(BF)
        stage[owner, 256:272, :] = stats.astype(BF)

        @pl.when(owner != me)
        def _():
            s_copy(owner, me).start()

    @pl.loop(0, PLANE // 2)
    def _(i):
        group = lax.rem(row_x + lax.div(i, 2), 4)
        first = lax.rem(row_y + 2 * lax.rem(i, 2), 4)
        second = lax.rem(first + 1, 4)

        @pl.when(jnp.logical_and(i < 2, i > 0))
        def _():
            arrange(first)

        @pl.when(i < 2)
        def _():
            arrange(second)

        @pl.when(i == 1)
        def _():
            f_copy(row_x, lax.rem(row_x + 2, 4)).start()

        @pl.when(jnp.logical_and(i > 0, lax.rem(i, 2) == 0))
        def _():
            f_copy(group, row_x).wait_recv()

        score(first, group, scores_a)
        score(second, group, scores_b)
        level_a, total_a = soften(first, scores_a, probs_a)
        finish(first * 4 + group, first, probs_a, level_a, total_a)
        level_b, total_b = soften(second, scores_b, probs_b)
        finish(second * 4 + group, second, probs_b, level_b, total_b)

    recv[me] = stage[me]

    @pl.loop(1, PLANE)
    def _(i):
        s_copy(me, lax.rem(me + i, PLANE)).wait_recv()

    terms = recv[:, 256:272, :].astype(F32)
    term_iota = lax.broadcasted_iota(jnp.int32, (16, 16, 128), 1)
    columns = []
    for half in range(2):
        mine = jnp.logical_and(term_iota < 6, lax.rem(term_iota, 2) == half)
        level = jnp.sum(jnp.where(mine, terms, 0.0), axis=1)
        weight = jnp.exp2(level - jnp.max(level, axis=0, keepdims=True))
        weight = weight / jnp.sum(weight, axis=0, keepdims=True)
        padded = jnp.concatenate([weight, jnp.zeros((112, 128), F32)], axis=0)
        columns.append(jnp.transpose(padded))
    weights = jnp.concatenate(columns, axis=0)
    merged = jnp.zeros((256, 128), F32)
    for source in range(PLANE):
        merged = merged + weights[:, source : source + 1] * recv[source, 0:256, :].astype(F32)
    split[...] = merged.reshape(16, 16, 128)
    for head in range(16):
        flat[:, head * 128 : head * 128 + 128] = split[:, head, :].astype(BF)

    left, right = pl.ds(0, 1024), pl.ds(1024, 1024)

    def a_copy(axis, source, target):
        if axis == 0:
            spot, cols, device = (source, row_y), left, (z, c, target * 4 + row_y)
        else:
            spot, cols, device = (row_x, source), right, (z, c, row_x * 4 + target)
        return remote(
            flat.at[:, cols],
            abuf.at[spot[0], spot[1], :, cols],
            a_send.at[axis, target],
            a_recv.at[axis, source],
            device,
        )

    def b_copy(axis, source, target):
        if axis == 0:
            block, device = abuf.at[:, source, :, left], (z, c, row_x * 4 + target)
        else:
            block, device = abuf.at[source, :, :, right], (z, c, target * 4 + row_y)
        return remote(block, block, b_send.at[axis, target], b_recv.at[axis, source], device)

    @pl.loop(1, 4)
    def _(i):
        a_copy(0, row_x, lax.rem(row_x + i, 4)).start()
        a_copy(1, row_y, lax.rem(row_y + i, 4)).start()

    abuf[row_x, row_y] = flat[...]

    @pl.loop(1, DEPTH)
    def _(i):
        m_copy(lax.rem(z + i, DEPTH), z).wait_recv()

    @pl.loop(1, 4)
    def _(i):
        a_copy(0, lax.rem(row_x + i, 4), row_x).wait_recv()

    @pl.loop(1, 4)
    def _(i):
        b_copy(0, row_y, lax.rem(row_y + i, 4)).start()

    @pl.loop(1, 4)
    def _(i):
        a_copy(1, lax.rem(row_y + i, 4), row_y).wait_recv()

    @pl.loop(1, 4)
    def _(i):
        b_copy(1, row_x, lax.rem(row_x + i, 4)).start()

    meta = jnp.sum(mbuf[...], axis=0)
    expert_iota = lax.broadcasted_iota(jnp.int32, (16, 128), 0).astype(F32)
    expert_iota = expert_iota + (z * PLANE).astype(F32)
    named = jnp.zeros((16, 128), F32)
    weight = jnp.zeros((16, 128), F32)
    for k in range(8):
        hit = meta[k : k + 1, :] == expert_iota
        named = named + jnp.where(hit, 1.0, 0.0)
        weight = weight + jnp.where(hit, meta[8 + k : 9 + k, :], 0.0)
    from_row = lax.broadcasted_iota(jnp.int32, (128, 128), 0)
    to_row = lax.broadcasted_iota(jnp.int32, (128, 128), 1)
    same = lax.div(from_row, 16) == lax.div(to_row, 16)
    earlier = jnp.where(jnp.logical_and(same, from_row < to_row), 1.0, 0.0).astype(BF)
    rank = jnp.dot(named.astype(BF), earlier, preferred_element_type=F32)
    slot = 2.0 * lax.div(lax.broadcasted_iota(jnp.int32, (16, 128), 1), 16).astype(F32) + rank
    slot = jnp.where(named > 0.5, slot, -1.0)
    slot_iota = lax.broadcasted_iota(jnp.int32, (16, 16, 128), 1).astype(F32)
    chosen = slot[:, None, :] == slot_iota
    placing = jnp.where(chosen, 1.0, 0.0).reshape(256, 128).astype(BF)
    scaled = jnp.where(chosen, weight[:, None, :], 0.0).reshape(256, 128)
    turned = jnp.transpose(scaled)
    turned_high = turned.astype(BF)
    turned_low = (turned - turned_high.astype(F32)).astype(BF)

    w_copy(0).wait()

    @pl.loop(1, 4)
    def _(i):
        b_copy(0, lax.rem(row_y + i, 4), row_y).wait_recv()
        b_copy(1, lax.rem(row_x + i, 4), row_x).wait_recv()

    projected = jnp.dot(abuf[...].reshape(256, 2048), w_ref[...], preferred_element_type=F32)
    pstage[...] = projected.reshape(16, 16, 128)
    own_side = lax.div(me, 8)

    def p_copy(source_core, source, target):
        return remote(
            pstage.at[target],
            pbuf.at[source_core, lax.rem(source, 8)],
            p_send.at[target],
            p_recv.at[source_core, lax.rem(source, 8)],
            (z, lax.div(source, 8), target),
        )

    @pl.loop(1, PLANE)
    def _(i):
        p_copy(c, me, lax.rem(me + i, PLANE)).start()

    @pl.when(own_side != c)
    def _():
        p_copy(c, me, me).start()

    @pl.when(own_side == c)
    def _():
        pbuf[c, lax.rem(me, 8)] = pstage[me]

    @pl.loop(0, 8)
    def _(i):
        p_copy(other, c * 8 + i, me).wait_recv()

        @pl.when(c * 8 + i != me)
        def _():
            p_copy(c, c * 8 + i, me).wait_recv()

    mine = pl.ds(pl.multiple_of(c * 1024, 1024), 1024)
    theirs = pl.ds(pl.multiple_of(other * 1024, 1024), 1024)
    square = jnp.zeros((16, 128), F32)
    for part in range(8):
        cols = pl.ds(pl.multiple_of(c * 1024 + part * 128, 128), 128)
        hidden = res_ref[:, cols].astype(F32) + (pbuf[0, part] + pbuf[1, part])
        hid_ref[:, part * 128 : part * 128 + 128] = hidden
        square = square + hidden * hidden
    sq_stage[...] = square
    sq_copy = remote(sq_stage, sq_recv, sq_sems.at[0], sq_sems.at[1], (z, other, me))
    sq_copy.start()
    scaled_hidden = hid_ref[...] * gain_ref[:, mine]
    sq_copy.wait_recv()
    square = square + sq_recv[...]
    mean_square = jnp.sum(square, axis=1, keepdims=True) * (1.0 / 2048.0)
    norm_ref[...] = (scaled_hidden * lax.rsqrt(mean_square + norm_epsilon)).astype(BF)

    def z_copy(source, target):
        return remote(
            norm_ref, zbuf.at[rows16(source), :], z_send.at[target], z_recv.at[source], (target, c, me)
        )

    @pl.loop(1, DEPTH)
    def _(i):
        z_copy(z, lax.rem(z + i, DEPTH)).start()

    zbuf[rows16(z), :] = norm_ref[...]
    w_copy(1).wait()

    @pl.loop(0, 2048 // TURN)
    def _(i):
        rows = pl.ds(pl.multiple_of(i * TURN, TURN), TURN)
        for side in range(2):
            in_ref[rows, side * 384 : side * 384 + 384] = in_raw[rows, side, :]

    w_copy(2).wait()

    @pl.loop(1, DEPTH)
    def _(i):
        z_copy(lax.rem(z + i, DEPTH), z).wait_recv()

    xstage[...] = jnp.dot(placing, zbuf[...], preferred_element_type=F32).astype(BF)

    def x_copy(source, target):
        return remote(
            xstage.at[rows16(target), :],
            xbuf.at[rows16(source), mine],
            x_send.at[target],
            x_recv.at[source],
            (z, c, target),
        )

    def h_copy(source, columns):
        return remote(
            xbuf.at[rows16(source), columns],
            xbuf.at[rows16(source), columns],
            h_send.at[source],
            h_recv.at[source],
            (z, other, me),
        )

    @pl.loop(1, PLANE)
    def _(i):
        x_copy(me, lax.rem(me + i, PLANE)).start()

    xbuf[rows16(me), mine] = xstage[rows16(me), :]
    h_copy(me, mine).start()

    @pl.loop(1, PLANE)
    def _(i):
        peer = lax.rem(me + PLANE - i, PLANE)
        x_copy(peer, me).wait_recv()
        h_copy(peer, mine).start()

    @pl.loop(0, PLANE)
    def _(i):
        h_copy(i, theirs).wait_recv()

    gate_up = jnp.dot(xbuf[...], in_ref[...], preferred_element_type=F32)
    gate = gate_up[:, :384]
    active = (gate / (1.0 + jnp.exp(-gate)) * gate_up[:, 384:]).astype(BF)
    ystage[...] = jnp.dot(active, down_ref[:, theirs], preferred_element_type=F32).astype(BF)
    y_copy = remote(ystage, ybuf, y_sems.at[0], y_sems.at[1], (z, other, me))
    y_copy.start()
    own = jnp.dot(active, down_ref[:, mine], preferred_element_type=F32)
    y_copy.wait_recv()
    rstage[...] = (own + ybuf[...].astype(F32)).astype(BF)

    def r_copy(source, target):
        return remote(
            rstage.at[rows16(target), :],
            rbuf.at[rows16(source), :],
            r_send.at[target],
            r_recv.at[source],
            (z, c, target),
        )

    @pl.loop(1, PLANE)
    def _(i):
        r_copy(me, lax.rem(me + i, PLANE)).start()

    rbuf[rows16(me), :] = rstage[rows16(me), :]

    @pl.loop(1, PLANE)
    def _(i):
        r_copy(lax.rem(me + i, PLANE), me).wait_recv()

    mixed = jnp.dot(turned_high, rbuf[...], preferred_element_type=F32)
    mixed = mixed + jnp.dot(turned_low, rbuf[...], preferred_element_type=F32)
    cstage[...] = mixed.astype(BF)

    def c_copy(source, target):
        return remote(
            cstage.at[rows16(target), :],
            cbuf.at[source],
            c_send.at[target],
            c_recv.at[source],
            (target, c, me),
        )

    @pl.loop(1, DEPTH)
    def _(i):
        c_copy(z, lax.rem(z + i, DEPTH)).start()

    cbuf[z] = cstage[rows16(z), :]

    @pl.loop(1, DEPTH)
    def _(i):
        c_copy(lax.rem(z + i, DEPTH), z).wait_recv()

    total = hid_ref[...]
    for source in range(DEPTH):
        total = total + cbuf[source].astype(F32)
    out_ref[...] = total.astype(BF)

    @pl.loop(1, 4)
    def _(i):
        side_x, side_y = lax.rem(row_x + i, 4), lax.rem(row_y + i, 4)
        q_copy(row_y, side_y).wait_send()
        f_copy(row_x, side_x).wait_send()
        a_copy(0, row_x, side_x).wait_send()
        a_copy(1, row_y, side_y).wait_send()
        b_copy(0, row_y, side_y).wait_send()
        b_copy(1, row_x, side_x).wait_send()

    @pl.loop(1, PLANE)
    def _(i):
        peer = lax.rem(me + i, PLANE)
        s_copy(peer, me).wait_send()
        p_copy(c, me, peer).wait_send()
        x_copy(me, peer).wait_send()
        r_copy(me, peer).wait_send()

    @pl.when(own_side != c)
    def _():
        p_copy(c, me, me).wait_send()

    @pl.loop(0, PLANE)
    def _(i):
        h_copy(i, mine).wait_send()

    sq_copy.wait_send()
    y_copy.wait_send()

    @pl.loop(1, DEPTH)
    def _(i):
        peer = lax.rem(z + i, DEPTH)
        m_copy(z, peer).wait_send()
        z_copy(z, peer).wait_send()
        c_copy(z, peer).wait_send()


def dma(*shape):
    return pltpu.SemaphoreType.DMA(shape)


def layer(span, *operands):
    specs = [pl.BlockSpec(memory_space=pltpu.VMEM)] * 13
    for held in (3, 4, 7, 11, 12):
        specs[held] = pl.BlockSpec(memory_space=pl.ANY)
    specs[5] = pl.BlockSpec(memory_space=pltpu.SMEM)
    keys = span + 128
    return pl.pallas_call(
        functools.partial(layer_kernel, span),
        out_shape=jax.ShapeDtypeStruct((16, 1024), BF),
        in_specs=specs,
        out_specs=pl.BlockSpec(memory_space=pltpu.VMEM),
        scratch_shapes=[
            pltpu.VMEM((2, 4, 2 * span, 128), BF),
            pltpu.VMEM((2 * TILE, 128), F32),
            pltpu.VMEM((4, keys, 256), BF),
            pltpu.VMEM((4, keys, 256), BF),
            pltpu.VMEM((4, 8, keys), F32),
            pltpu.VMEM((4, 1024, 128), BF),
            pltpu.VMEM((256, keys), F32),
            pltpu.VMEM((256, keys), F32),
            pltpu.VMEM((256, keys), BF),
            pltpu.VMEM((256, keys), BF),
            pltpu.VMEM((PLANE, 272, 128), BF),
            pltpu.VMEM((PLANE, 272, 128), BF),
            pltpu.VMEM((16, 16, 128), F32),
            pltpu.VMEM((16, 2048), BF),
            pltpu.VMEM((4, 4, 16, 2048), BF),
            pltpu.VMEM((2048, 128), BF),
            pltpu.VMEM((16, 16, 128), F32),
            pltpu.VMEM((2, 8, 16, 128), F32),
            pltpu.VMEM((16, 1024), F32),
            pltpu.VMEM((16, 128), F32),
            pltpu.VMEM((16, 128), F32),
            pltpu.VMEM((16, 1024), BF),
            pltpu.VMEM((2048, 2, 384), BF),
            pltpu.VMEM((2048, 768), BF),
            pltpu.VMEM((384, 2048), BF),
            pltpu.VMEM((16, 128), F32),
            pltpu.VMEM((128, 1024), BF),
            pltpu.VMEM((DEPTH, 16, 128), F32),
            pltpu.VMEM((256, 1024), BF),
            pltpu.VMEM((256, 2048), BF),
            pltpu.VMEM((256, 1024), BF),
            pltpu.VMEM((256, 1024), BF),
            pltpu.VMEM((256, 1024), BF),
            pltpu.VMEM((256, 1024), BF),
            pltpu.VMEM((128, 1024), BF),
            pltpu.VMEM((DEPTH, 16, 1024), BF),
            dma(2, 4),
            dma(3),
            dma(4),
            dma(4),
            dma(4),
            dma(4),
            dma(PLANE),
            dma(PLANE),
            dma(2, 4),
            dma(2, 4),
            dma(2, 4),
            dma(2, 4),
            dma(PLANE),
            dma(2, 8),
            dma(2),
            dma(DEPTH),
            dma(DEPTH),
            dma(DEPTH),
            dma(DEPTH),
            dma(PLANE),
            dma(PLANE),
            dma(PLANE),
            dma(PLANE),
            dma(2),
            dma(PLANE),
            dma(PLANE),
            dma(DEPTH),
            dma(DEPTH),
        ],
        compiler_params=pltpu.CompilerParams(
            collective_id=0, has_side_effects=True, vmem_limit_bytes=VMEM_LIMIT
        ),
    )(*operands)


def local(
    queries,
    new_keys,
    new_values,
    key_cache,
    value_cache,
    lengths,
    residual,
    out_weight,
    norm_gain,
    route_ids,
    route_weights,
    expert_in,
    expert_out,
):
    requests, span = key_cache.shape[:2]
    return layer(
        span,
        queries.reshape(requests, 64, 128),
        new_keys.reshape(requests, 8, 128),
        new_values.reshape(requests, 8, 128),
        key_cache.reshape(requests, 2 * span, 128),
        value_cache.reshape(requests, 2 * span, 128),
        lengths,
        residual,
        out_weight,
        norm_gain.reshape(1, -1),
        route_ids.T,
        route_weights.T,
        expert_in.reshape(2048, 2, 384),
        expert_out.reshape(384, 2048),
    )


def solution(mesh):
    return jax.shard_map(
        local,
        mesh=mesh,
        in_specs=(
            P("req", "exp", "head", None),
            P("req", "exp", "head", None),
            P("req", "exp", "head", None),
            P("req", "exp", "head", None),
            P("req", "exp", "head", None),
            P("req"),
            P(("req", "exp"), None),
            P("head", "exp"),
            P(),
            P(("req", "exp"), None),
            P(("req", "exp"), None),
            P(("req", "exp"), None, None, "head"),
            P(("req", "exp"), "head", None),
        ),
        out_specs=P(("req", "exp"), "head"),
        check_vma=False,
    )
```

time: 441 us -> 113 us (0.26)
  waiting for transfers between devices: 196 us -> 0 us
  blocking collectives: 130 us -> 0 us
  Pallas kernels: 0 us -> 110 us
  matrix products: 30.5 us -> 0 us
  local copies, waits for them, and re-layouts: 29.7 us -> 1.38 us
  starting transfers between devices: 27 us -> 0 us
  other arithmetic: 13.8 us -> 0 us
  between operations: 13.4 us -> 0.01 us
    pallas_call x0 -> x1, Pallas kernels: none -> 110 us  [layer(): pl.pallas_call(functools.partial(layer_kernel, span), out_shape=jax.Shape...]
    all_to_all x3 -> x0, waiting for transfers between devices: 74.2 us -> none  [the longest x1 47.1 us: local(): lax.all_to_all(partial_value, ('req', 'exp'), split_axis=0, concat_axis=0...]
    psum x2 -> x0, blocking collectives: 71.5 us -> none  [the longest x1 55.6 us: local(): all_sums, all_totals = lax.psum((weighted, totals), 'exp')]
    psum x2 -> x0, waiting for transfers between devices: 69.8 us -> none  [the longest x1 41.2 us: local(): all_sums, all_totals = lax.psum((weighted, totals), 'exp')]
    pmax x1 -> x0, blocking collectives: 58.3 us -> none  [local(): row_max = lax.pmax(local_max, 'exp')]
    all_gather x1 -> x0, waiting for transfers between devices: 51 us -> none  [local(): whole_queries = lax.all_gather(queries, 'exp', axis=1, tiled=True)]
    dot_general x8 -> x0, matrix products: 30.5 us -> none  [the longest x1 10.8 us: local(): jnp.einsum('rkgbs,rskd->rbkgd', cache_exp.astype(jnp.bfloat16), value_cac...]
    all_to_all x3 -> x0, starting transfers between devices: 26.9 us -> none  [the longest x1 11.4 us: local(): lax.all_to_all(outgoing, ('req', 'exp'), split_axis=0, concat_axis=0, til...]
  transfers between devices with their start and end apart: 6 -> 0, of which waited for: 6 -> 0; matrix products, arithmetic and copies ran while one was open for 6% -> 0% of each run, Pallas kernels for 0% -> 0%
where the time goes in v2:
time: 113 us; the launch traced here: 111 us
  Pallas kernels  110 us (97%)
  local copies, waits for them, and re-layouts  1.38 us (1%)
    pallas_call x1, Pallas kernels, layer(): pl.pallas_call(functools.partial(layer_kernel, span), out_shape=jax.Shape...  110 us

profile of v2, /device:TPU:1, one launch (start us, length us, event | category | flops | bytes accessed | tf_op | source)
XLA Modules:
  0.0 111.3 jit_solution(10669665473933513247)
XLA Ops:
  0.0 109.9 %shard_map.127 = bf16[16,1024]{1,0:T(8,128)(2,1)} custom-call(bf16[4,64,128]{2,1,0:T(8,128)(2,1)} %bitcast.14, bf16[4,8,128]{2,1,0:T(8,128)(2,1)} %bitcast.15, bf16[4,8,128]{2,1,0:T(8,128)(2,1)} %bitcast.16, bf16[4,3072,128]{2,1,0:T(8,128)(2,1)} %bitcast.10, bf16[4,3072,128]{2,1,0:T(8,128)(2,1)} %bitcast.11, s32[4]{0:T(128)} %len_ref.1, ...), custom_call_target="tpu_custom_call" | custom-call | tf_op jit(solution)/shard_map/pallas_call | solution.py:648
  110.0 1.4 %copy.15 = bf16[16,1024]{1,0:T(8,128)(2,1)} copy(bf16[16,1024]{1,0:T(8,128)(2,1)} %shard_map.127) | data formatting | bytes 65536

commit v3 on v2

--- a/solution.py
+++ b/solution.py
@@ -85,6 +85,7 @@
     mbuf,
     xstage,
     xbuf,
+    own_ref,
     ystage,
     ybuf,
     rstage,
@@ -114,17 +115,37 @@
     x_recv,
     h_send,
     h_recv,
-    y_sems,
+    y_send,
+    y_recv,
     r_send,
     r_recv,
     c_send,
     c_recv,
 ):
+    after = []
     z, c, me = place()
     other = 1 - c
     row_x = lax.div(me, 4)
     row_y = lax.rem(me, 4)
 
+    sign = 1 - 2 * lax.rem(row_x + row_y, 2)
+
+    def moved(way, step_x, step_y):
+        return lax.rem(row_x + way * step_x + 4, 4), lax.rem(row_y + way * step_y + 4, 4)
+
+    def steps(k):
+        step_x = lax.rem(k, 4)
+        return step_x, lax.rem(step_x + lax.div(k, 4), 4)
+
+    def partner(k):
+        to_x, to_y = moved(sign, *steps(k))
+        return to_x * 4 + to_y
+
+    def origin(k):
+        step_x, step_y = steps(k)
+        from_x, from_y = moved(sign * (2 * lax.rem(step_x + step_y, 2) - 1), step_x, step_y)
+        return from_x * 4 + from_y
+
     def kv_copy(which, request):
         source = (k_hbm, v_hbm)[which]
         return pltpu.make_async_copy(
@@ -135,15 +156,6 @@
         source, target = ((w_hbm, w_ref), (in_hbm, in_raw), (down_hbm, down_ref))[which]
         return pltpu.make_async_copy(source, target, w_sems.at[which])
 
-    @pl.loop(0, 4)
-    def _(i):
-        request = lax.rem(row_y + i, 4)
-        kv_copy(0, request).start()
-        kv_copy(1, request).start()
-
-    for which in range(3):
-        w_copy(which).start()
-
     barrier = pltpu.get_barrier_semaphore()
 
     def greet(*target):
@@ -160,24 +172,48 @@
         greet(lax.rem(z + i, DEPTH), c, me)
 
     greet(z, other, me)
+
+    @pl.loop(0, 4)
+    def _(i):
+        request = lax.rem(2 + i, 4)
+        kv_copy(0, request).start()
+        kv_copy(1, request).start()
+
+    for which in range(3):
+        w_copy(which).start()
+
     meta_ref[...] = jnp.zeros((16, 128), F32)
     meta_ref[0:8, 0:16] = ids_ref[...].astype(F32)
     meta_ref[8:16, 0:16] = wts_ref[...]
     meta_ref[...] = pltpu.roll(meta_ref[...], 16 * z, 1)
     pl.semaphore_wait(barrier, 2 * PLANE - 1 + DEPTH - 1)
 
-    def q_copy(source, target):
-        return remote(
-            q_ref,
-            qbuf.at[:, pl.ds(pl.multiple_of((row_x * 4 + source) * 64, 64), 64), :],
-            q_send.at[target],
-            q_recv.at[source],
-            (z, c, row_x * 4 + target),
-        )
-
-    @pl.loop(1, 4)
-    def _(i):
-        q_copy(row_y, lax.rem(row_y + i, 4)).start()
+    def q_copy(axis, source, target):
+        span_rows = pl.ds(2 * axis, 2)
+        if axis == 0:
+            block, device = (source, row_y), (z, c, target * 4 + row_y)
+        else:
+            block, device = (row_x, source), (z, c, row_x * 4 + target)
+        cols = pl.ds(pl.multiple_of(block[1] * 64, 64), 64)
+        return remote(
+            q_ref.at[span_rows],
+            qbuf.at[span_rows, block[0], cols, :],
+            q_send.at[axis, target],
+            q_recv.at[axis, source],
+            device,
+        )
+
+    @pl.loop(1, 4)
+    def _(i):
+        q_copy(1, row_y, lax.rem(row_y + i, 4)).start()
+        q_copy(0, row_x, lax.rem(row_x + i, 4)).start()
+
+    @after.append
+    def _():
+        @pl.loop(1, 4)
+        def _(i):
+            q_copy(0, row_x, lax.rem(row_x + i, 4)).wait_send()
+            q_copy(1, row_y, lax.rem(row_y + i, 4)).wait_send()
 
     def m_copy(source, target):
         return remote(
@@ -188,18 +224,22 @@
     def _(i):
         m_copy(z, lax.rem(z + i, DEPTH)).start()
 
+    @after.append
+    def _():
+        @pl.loop(1, DEPTH)
+        def _(i):
+            m_copy(z, lax.rem(z + i, DEPTH)).wait_send()
+
     mbuf[z] = meta_ref[...]
-    qbuf[:, pl.ds(pl.multiple_of(me * 64, 64), 64), :] = q_ref[...]
-
-    def f_copy(source, target):
-        rows = pl.ds(pl.multiple_of(source * 256, 256), 256)
-        return remote(
-            qbuf.at[:, rows, :],
-            qbuf.at[:, rows, :],
-            f_send.at[target],
-            f_recv.at[source],
-            (z, c, target * 4 + row_y),
-        )
+    qbuf[:, row_x, pl.ds(pl.multiple_of(row_y * 64, 64), 64), :] = q_ref[...]
+
+    def f_copy(axis, source, target):
+        if axis == 0:
+            cols = pl.ds(pl.multiple_of(source * 64, 64), 64)
+            block, device = qbuf.at[0:2, :, cols, :], (z, c, row_x * 4 + target)
+        else:
+            block, device = qbuf.at[2:4, source, :, :], (z, c, target * 4 + row_y)
+        return remote(block, block, f_send.at[axis, target], f_recv.at[axis, source], device)
 
     keys = span + 128
     key_iota = lax.broadcasted_iota(jnp.int32, (8, keys), 1)
@@ -227,14 +267,39 @@
             target[request, tail, 0:128] = loose[pl.ds(0, 128, 2), :].astype(BF)
             target[request, tail, 128:256] = loose[pl.ds(1, 128, 2), :].astype(BF)
 
-    arrange(row_y)
-
-    @pl.loop(1, 4)
-    def _(i):
-        q_copy(lax.rem(row_y + i, 4), row_y).wait_recv()
-
-    f_copy(row_x, lax.rem(row_x + 3, 4)).start()
-    f_copy(row_x, lax.rem(row_x + 1, 4)).start()
+    arrange(2)
+
+    @pl.loop(1, 4)
+    def _(i):
+        q_copy(1, lax.rem(row_y + i, 4), row_y).wait_recv()
+
+    @pl.loop(1, 4)
+    def _(i):
+        f_copy(1, row_x, lax.rem(row_x + i, 4)).start()
+
+    @pl.loop(1, 4)
+    def _(i):
+        q_copy(0, lax.rem(row_x + i, 4), row_x).wait_recv()
+
+    @pl.loop(1, 4)
+    def _(i):
+        f_copy(0, row_y, lax.rem(row_y + i, 4)).start()
+
+    @after.append
+    def _():
+        @pl.loop(1, 4)
+        def _(i):
+            f_copy(0, row_y, lax.rem(row_y + i, 4)).wait_send()
+            f_copy(1, row_x, lax.rem(row_x + i, 4)).wait_send()
+
+    arrange(3)
+    arrange(0)
+    arrange(1)
+
+    @pl.loop(1, 4)
+    def _(i):
+        f_copy(1, lax.rem(row_x + i, 4), row_x).wait_recv()
+        f_copy(0, lax.rem(row_y + i, 4), row_y).wait_recv()
 
     row_iota = lax.broadcasted_iota(jnp.int32, (256, 128), 0)
     low = lax.rem(row_iota, 16) < 8
@@ -254,7 +319,7 @@
         )
 
     def score(request, group, scores):
-        q = qbuf[request, pl.ds(pl.multiple_of(group * 256, 256), 256), :]
+        q = qbuf[request, group]
         both = jnp.concatenate([q * low_mask, q * high_mask], axis=1)
         scores[...] = lax.dot_general(
             both, k_ref[request], (((1,), (1,)), ((), ())), preferred_element_type=F32
@@ -297,34 +362,23 @@
         def _():
             s_copy(owner, me).start()
 
+    @after.append
+    def _():
+        @pl.loop(1, PLANE)
+        def _(i):
+            s_copy(lax.rem(me + i, PLANE), me).wait_send()
+
     @pl.loop(0, PLANE // 2)
     def _(i):
-        group = lax.rem(row_x + lax.div(i, 2), 4)
-        first = lax.rem(row_y + 2 * lax.rem(i, 2), 4)
-        second = lax.rem(first + 1, 4)
-
-        @pl.when(jnp.logical_and(i < 2, i > 0))
-        def _():
-            arrange(first)
-
-        @pl.when(i < 2)
-        def _():
-            arrange(second)
-
-        @pl.when(i == 1)
-        def _():
-            f_copy(row_x, lax.rem(row_x + 2, 4)).start()
-
-        @pl.when(jnp.logical_and(i > 0, lax.rem(i, 2) == 0))
-        def _():
-            f_copy(group, row_x).wait_recv()
-
-        score(first, group, scores_a)
-        score(second, group, scores_b)
-        level_a, total_a = soften(first, scores_a, probs_a)
-        finish(first * 4 + group, first, probs_a, level_a, total_a)
-        level_b, total_b = soften(second, scores_b, probs_b)
-        finish(second * 4 + group, second, probs_b, level_b, total_b)
+        step_x = lax.rem(lax.div(i, 2) + 1, 4)
+        request, group_a = moved(sign, step_x, 2 + lax.rem(i, 2))
+        group_b = moved(sign, step_x, 1 - lax.rem(i, 2))[1]
+        score(request, group_a, scores_a)
+        score(request, group_b, scores_b)
+        level_a, total_a = soften(request, scores_a, probs_a)
+        finish(request * 4 + group_a, request, probs_a, level_a, total_a)
+        level_b, total_b = soften(request, scores_b, probs_b)
+        finish(request * 4 + group_b, request, probs_b, level_b, total_b)
 
     recv[me] = stage[me]
 
@@ -377,6 +431,13 @@
         a_copy(0, row_x, lax.rem(row_x + i, 4)).start()
         a_copy(1, row_y, lax.rem(row_y + i, 4)).start()
 
+    @after.append
+    def _():
+        @pl.loop(1, 4)
+        def _(i):
+            a_copy(0, row_x, lax.rem(row_x + i, 4)).wait_send()
+            a_copy(1, row_y, lax.rem(row_y + i, 4)).wait_send()
+
     abuf[row_x, row_y] = flat[...]
 
     @pl.loop(1, DEPTH)
@@ -398,6 +459,13 @@
     @pl.loop(1, 4)
     def _(i):
         b_copy(1, row_x, lax.rem(row_x + i, 4)).start()
+
+    @after.append
+    def _():
+        @pl.loop(1, 4)
+        def _(i):
+            b_copy(0, row_y, lax.rem(row_y + i, 4)).wait_send()
+            b_copy(1, row_x, lax.rem(row_x + i, 4)).wait_send()
 
     meta = jnp.sum(mbuf[...], axis=0)
     expert_iota = lax.broadcasted_iota(jnp.int32, (16, 128), 0).astype(F32)
@@ -445,11 +513,23 @@
 
     @pl.loop(1, PLANE)
     def _(i):
-        p_copy(c, me, lax.rem(me + i, PLANE)).start()
+        p_copy(c, me, partner(i)).start()
 
     @pl.when(own_side != c)
     def _():
         p_copy(c, me, me).start()
+
+    @after.append
+    def _():
+        @pl.loop(1, PLANE)
+        def _(i):
+            p_copy(c, me, lax.rem(me + i, PLANE)).wait_send()
+
+    @after.append
+    def _():
+        @pl.when(own_side != c)
+        def _():
+            p_copy(c, me, me).wait_send()
 
     @pl.when(own_side == c)
     def _():
@@ -474,6 +554,7 @@
     sq_stage[...] = square
     sq_copy = remote(sq_stage, sq_recv, sq_sems.at[0], sq_sems.at[1], (z, other, me))
     sq_copy.start()
+    after.append(sq_copy.wait_send)
     scaled_hidden = hid_ref[...] * gain_ref[:, mine]
     sq_copy.wait_recv()
     square = square + sq_recv[...]
@@ -489,6 +570,12 @@
     def _(i):
         z_copy(z, lax.rem(z + i, DEPTH)).start()
 
+    @after.append
+    def _():
+        @pl.loop(1, DEPTH)
+        def _(i):
+            z_copy(z, lax.rem(z + i, DEPTH)).wait_send()
+
     zbuf[rows16(z), :] = norm_ref[...]
     w_copy(1).wait()
 
@@ -506,69 +593,101 @@
 
     xstage[...] = jnp.dot(placing, zbuf[...], preferred_element_type=F32).astype(BF)
 
-    def x_copy(source, target):
+    def x_copy(step):
+        target = partner(step)
         return remote(
             xstage.at[rows16(target), :],
-            xbuf.at[rows16(source), mine],
-            x_send.at[target],
-            x_recv.at[source],
+            xbuf.at[rows16(step), mine],
+            x_send.at[step],
+            x_recv.at[step],
             (z, c, target),
         )
 
-    def h_copy(source, columns):
-        return remote(
-            xbuf.at[rows16(source), columns],
-            xbuf.at[rows16(source), columns],
-            h_send.at[source],
-            h_recv.at[source],
-            (z, other, me),
-        )
+    def h_copy(step, columns):
+        block = xbuf.at[rows16(step), columns]
+        return remote(block, block, h_send.at[step], h_recv.at[step], (z, other, me))
+
+    def y_copy(half):
+        rows = pl.ds(half * 128, 128)
+        return remote(
+            ystage.at[rows, :], ybuf.at[rows, :], y_send.at[half], y_recv.at[half], (z, other, me)
+        )
+
+    def r_copy(step, expert):
+        return remote(
+            rstage.at[rows16(step), :],
+            rbuf.at[rows16(expert), :],
+            r_send.at[step],
+            r_recv.at[step],
+            (z, c, origin(step)),
+        )
+
+    def forward(start, stop):
+        @pl.loop(start, stop)
+        def _(i):
+            x_copy(i).wait_recv()
+            h_copy(i, mine).start()
+
+    def evaluate(half):
+        @pl.loop(8 * half, 8 * half + 8)
+        def _(i):
+            h_copy(i, theirs).wait_recv()
+
+        rows = slice(128 * half, 128 * half + 128)
+        gate_up = jnp.dot(xbuf[rows, :], in_ref[...], preferred_element_type=F32)
+        gate = gate_up[:, :384]
+        active = (gate / (1.0 + jnp.exp(-gate)) * gate_up[:, 384:]).astype(BF)
+        partial = jnp.dot(active, down_ref[:, theirs], preferred_element_type=F32)
+        ystage[rows, :] = partial.astype(BF)
+        y_copy(half).start()
+        own_ref[rows, :] = jnp.dot(active, down_ref[:, mine], preferred_element_type=F32)
+
+    def give_back(half):
+        rows = slice(128 * half, 128 * half + 128)
+        y_copy(half).wait_recv()
+        rstage[rows, :] = (own_ref[rows, :] + ybuf[rows, :].astype(F32)).astype(BF)
+
+        @pl.loop(max(1, 8 * half), 8 * half + 8)
+        def _(i):
+            r_copy(i, me).start()
 
     @pl.loop(1, PLANE)
     def _(i):
-        x_copy(me, lax.rem(me + i, PLANE)).start()
-
-    xbuf[rows16(me), mine] = xstage[rows16(me), :]
-    h_copy(me, mine).start()
+        x_copy(i).start()
+
+    @after.append
+    def _():
+        @pl.loop(1, PLANE)
+        def _(i):
+            x_copy(i).wait_send()
+
+    @after.append
+    def _():
+        @pl.loop(0, PLANE)
+        def _(i):
+            h_copy(i, mine).wait_send()
+
+    xbuf[0:16, mine] = xstage[rows16(me), :]
+    h_copy(0, mine).start()
+    forward(1, 8)
+    evaluate(0)
+    forward(8, PLANE)
+    give_back(0)
+    after.append(y_copy(0).wait_send)
+    after.append(y_copy(1).wait_send)
+    @after.append
+    def _():
+        @pl.loop(1, PLANE)
+        def _(i):
+            r_copy(i, me).wait_send()
+
+    rbuf[rows16(me), :] = rstage[0:16, :]
+    evaluate(1)
+    give_back(1)
 
     @pl.loop(1, PLANE)
     def _(i):
-        peer = lax.rem(me + PLANE - i, PLANE)
-        x_copy(peer, me).wait_recv()
-        h_copy(peer, mine).start()
-
-    @pl.loop(0, PLANE)
-    def _(i):
-        h_copy(i, theirs).wait_recv()
-
-    gate_up = jnp.dot(xbuf[...], in_ref[...], preferred_element_type=F32)
-    gate = gate_up[:, :384]
-    active = (gate / (1.0 + jnp.exp(-gate)) * gate_up[:, 384:]).astype(BF)
-    ystage[...] = jnp.dot(active, down_ref[:, theirs], preferred_element_type=F32).astype(BF)
-    y_copy = remote(ystage, ybuf, y_sems.at[0], y_sems.at[1], (z, other, me))
-    y_copy.start()
-    own = jnp.dot(active, down_ref[:, mine], preferred_element_type=F32)
-    y_copy.wait_recv()
-    rstage[...] = (own + ybuf[...].astype(F32)).astype(BF)
-
-    def r_copy(source, target):
-        return remote(
-            rstage.at[rows16(target), :],
-            rbuf.at[rows16(source), :],
-            r_send.at[target],
-            r_recv.at[source],
-            (z, c, target),
-        )
-
-    @pl.loop(1, PLANE)
-    def _(i):
-        r_copy(me, lax.rem(me + i, PLANE)).start()
-
-    rbuf[rows16(me), :] = rstage[rows16(me), :]
-
-    @pl.loop(1, PLANE)
-    def _(i):
-        r_copy(lax.rem(me + i, PLANE), me).wait_recv()
+        r_copy(i, partner(i)).wait_recv()
 
     mixed = jnp.dot(turned_high, rbuf[...], preferred_element_type=F32)
     mixed = mixed + jnp.dot(turned_low, rbuf[...], preferred_element_type=F32)
@@ -587,6 +706,12 @@
     def _(i):
         c_copy(z, lax.rem(z + i, DEPTH)).start()
 
+    @after.append
+    def _():
+        @pl.loop(1, DEPTH)
+        def _(i):
+            c_copy(z, lax.rem(z + i, DEPTH)).wait_send()
+
     cbuf[z] = cstage[rows16(z), :]
 
     @pl.loop(1, DEPTH)
@@ -598,41 +723,8 @@
         total = total + cbuf[source].astype(F32)
     out_ref[...] = total.astype(BF)
 
-    @pl.loop(1, 4)
-    def _(i):
-        side_x, side_y = lax.rem(row_x + i, 4), lax.rem(row_y + i, 4)
-        q_copy(row_y, side_y).wait_send()
-        f_copy(row_x, side_x).wait_send()
-        a_copy(0, row_x, side_x).wait_send()
-        a_copy(1, row_y, side_y).wait_send()
-        b_copy(0, row_y, side_y).wait_send()
-        b_copy(1, row_x, side_x).wait_send()
-
-    @pl.loop(1, PLANE)
-    def _(i):
-        peer = lax.rem(me + i, PLANE)
-        s_copy(peer, me).wait_send()
-        p_copy(c, me, peer).wait_send()
-        x_copy(me, peer).wait_send()
-        r_copy(me, peer).wait_send()
-
-    @pl.when(own_side != c)
-    def _():
-        p_copy(c, me, me).wait_send()
-
-    @pl.loop(0, PLANE)
-    def _(i):
-        h_copy(i, mine).wait_send()
-
-    sq_copy.wait_send()
-    y_copy.wait_send()
-
-    @pl.loop(1, DEPTH)
-    def _(i):
-        peer = lax.rem(z + i, DEPTH)
-        m_copy(z, peer).wait_send()
-        z_copy(z, peer).wait_send()
-        c_copy(z, peer).wait_send()
+    for settle in after:
+        settle()
 
 
 def dma(*shape):
@@ -656,7 +748,7 @@
             pltpu.VMEM((4, keys, 256), BF),
             pltpu.VMEM((4, keys, 256), BF),
             pltpu.VMEM((4, 8, keys), F32),
-            pltpu.VMEM((4, 1024, 128), BF),
+            pltpu.VMEM((4, 4, 256, 128), BF),
             pltpu.VMEM((256, keys), F32),
             pltpu.VMEM((256, keys), F32),
             pltpu.VMEM((256, keys), BF),
@@ -681,6 +773,7 @@
             pltpu.VMEM((DEPTH, 16, 128), F32),
             pltpu.VMEM((256, 1024), BF),
             pltpu.VMEM((256, 2048), BF),
+            pltpu.VMEM((256, 1024), F32),
             pltpu.VMEM((256, 1024), BF),
             pltpu.VMEM((256, 1024), BF),
             pltpu.VMEM((256, 1024), BF),
@@ -689,10 +782,10 @@
             pltpu.VMEM((DEPTH, 16, 1024), BF),
             dma(2, 4),
             dma(3),
-            dma(4),
-            dma(4),
-            dma(4),
-            dma(4),
+            dma(2, 4),
+            dma(2, 4),
+            dma(2, 4),
+            dma(2, 4),
             dma(PLANE),
             dma(PLANE),
             dma(2, 4),
@@ -710,6 +803,7 @@
             dma(PLANE),
             dma(PLANE),
             dma(PLANE),
+            dma(2),
             dma(2),
             dma(PLANE),
             dma(PLANE),

time: 113 us -> 107 us (0.947)
  Pallas kernels: 110 us -> 105 us
    pallas_call x1, Pallas kernels: 110 us -> 105 us  [layer(): pl.pallas_call(functools.partial(layer_kernel, span), out_shape=jax.Shape...]
where the time goes in v3:
time: 107 us; the launch traced here: 106 us
  Pallas kernels  105 us (98%)
  local copies, waits for them, and re-layouts  1.38 us (1%)
    pallas_call x1, Pallas kernels, layer(): pl.pallas_call(functools.partial(layer_kernel, span), out_shape=jax.Shape...  105 us

profile of v3, /device:TPU:1, one launch (start us, length us, event | category | flops | bytes accessed | tf_op | source)
XLA Modules:
  0.0 106.4 jit_solution(17800792508214165429)
XLA Ops:
  0.0 105.0 %shard_map.127 = bf16[16,1024]{1,0:T(8,128)(2,1)} custom-call(bf16[4,64,128]{2,1,0:T(8,128)(2,1)} %bitcast.14, bf16[4,8,128]{2,1,0:T(8,128)(2,1)} %bitcast.15, bf16[4,8,128]{2,1,0:T(8,128)(2,1)} %bitcast.16, bf16[4,3072,128]{2,1,0:T(8,128)(2,1)} %bitcast.10, bf16[4,3072,128]{2,1,0:T(8,128)(2,1)} %bitcast.11, s32[4]{0:T(128)} %len_ref.1, ...), custom_call_target="tpu_custom_call" | custom-call | tf_op jit(solution)/shard_map/pallas_call | solution.py:740
  105.0 1.4 %copy.15 = bf16[16,1024]{1,0:T(8,128)(2,1)} copy(bf16[16,1024]{1,0:T(8,128)(2,1)} %shard_map.127) | data formatting | bytes 65536

commit v4 on v3

--- a/solution.py
+++ b/solution.py
@@ -102,8 +102,10 @@
     s_recv,
     a_send,
     a_recv,
-    b_send,
-    b_recv,
+    g_send,
+    g_recv,
+    k_send,
+    k_recv,
     p_send,
     p_recv,
     sq_sems,
@@ -153,7 +155,8 @@
         )
 
     def w_copy(which):
-        source, target = ((w_hbm, w_ref), (in_hbm, in_raw), (down_hbm, down_ref))[which]
+        held = (w_ref.at[row_y], in_raw, down_ref)[which]
+        source, target = (w_hbm, in_hbm, down_hbm)[which], held
         return pltpu.make_async_copy(source, target, w_sems.at[which])
 
     barrier = pltpu.get_barrier_semaphore()
@@ -165,13 +168,14 @@
     def _(i):
         peer = lax.rem(me + i, PLANE)
         greet(z, c, peer)
-        greet(z, other, peer)
 
     @pl.loop(1, DEPTH)
     def _(i):
         greet(lax.rem(z + i, DEPTH), c, me)
 
-    greet(z, other, me)
+    @pl.loop(0, 4)
+    def _(i):
+        greet(z, other, i * 4 + row_y)
 
     @pl.loop(0, 4)
     def _(i):
@@ -186,7 +190,7 @@
     meta_ref[0:8, 0:16] = ids_ref[...].astype(F32)
     meta_ref[8:16, 0:16] = wts_ref[...]
     meta_ref[...] = pltpu.roll(meta_ref[...], 16 * z, 1)
-    pl.semaphore_wait(barrier, 2 * PLANE - 1 + DEPTH - 1)
+    pl.semaphore_wait(barrier, PLANE - 1 + 4 + DEPTH - 1)
 
     def q_copy(axis, source, target):
         span_rows = pl.ds(2 * axis, 2)
@@ -291,6 +295,44 @@
         def _(i):
             f_copy(0, row_y, lax.rem(row_y + i, 4)).wait_send()
             f_copy(1, row_x, lax.rem(row_x + i, 4)).wait_send()
+
+    def w_rows(side, batch):
+        return pl.ds(pl.multiple_of(lax.rem(side, 2) * 1024 + batch * 512, 512), 512)
+
+    def g_copy(source, target, batch):
+        return remote(
+            w_ref.at[source, w_rows(z, batch)],
+            w_ref.at[source, w_rows(z, batch)],
+            g_send.at[batch, target],
+            g_recv.at[batch, source],
+            (z, c, row_x * 4 + target),
+        )
+
+    def k_copy(side, part, batch):
+        rows = w_rows(side, batch)
+        return remote(
+            w_ref.at[part, rows],
+            w_ref.at[part, rows],
+            k_send.at[batch, part],
+            k_recv.at[batch, part],
+            (z + 1 - 2 * lax.rem(z, 2), c, me),
+        )
+
+    w_copy(0).wait()
+
+    for batch in range(2):
+
+        @pl.loop(1, 4)
+        def _(i):
+            g_copy(row_y, lax.rem(row_y + i, 4), batch).start()
+
+    @after.append
+    def _():
+        @pl.loop(1, 4)
+        def _(i):
+            for batch in range(2):
+                g_copy(row_y, lax.rem(row_y + i, 4), batch).wait_send()
+                k_copy(z, lax.rem(row_y + i, 4), batch).wait_send()
 
     arrange(3)
     arrange(0)
@@ -370,6 +412,15 @@
 
     @pl.loop(0, PLANE // 2)
     def _(i):
+        for batch in range(2):
+
+            @pl.when(i == 3 + 2 * batch)
+            def _():
+                @pl.loop(1, 4)
+                def _(k):
+                    g_copy(lax.rem(row_y + k, 4), row_y, batch).wait_recv()
+                    k_copy(z, lax.rem(row_y + k, 4), batch).start()
+
         step_x = lax.rem(lax.div(i, 2) + 1, 4)
         request, group_a = moved(sign, step_x, 2 + lax.rem(i, 2))
         group_b = moved(sign, step_x, 1 - lax.rem(i, 2))[1]
@@ -404,68 +455,30 @@
     for head in range(16):
         flat[:, head * 128 : head * 128 + 128] = split[:, head, :].astype(BF)
 
-    left, right = pl.ds(0, 1024), pl.ds(1024, 1024)
-
-    def a_copy(axis, source, target):
-        if axis == 0:
-            spot, cols, device = (source, row_y), left, (z, c, target * 4 + row_y)
-        else:
-            spot, cols, device = (row_x, source), right, (z, c, row_x * 4 + target)
-        return remote(
-            flat.at[:, cols],
-            abuf.at[spot[0], spot[1], :, cols],
-            a_send.at[axis, target],
-            a_recv.at[axis, source],
-            device,
-        )
-
-    def b_copy(axis, source, target):
-        if axis == 0:
-            block, device = abuf.at[:, source, :, left], (z, c, row_x * 4 + target)
-        else:
-            block, device = abuf.at[source, :, :, right], (z, c, target * 4 + row_y)
-        return remote(block, block, b_send.at[axis, target], b_recv.at[axis, source], device)
-
-    @pl.loop(1, 4)
-    def _(i):
-        a_copy(0, row_x, lax.rem(row_x + i, 4)).start()
-        a_copy(1, row_y, lax.rem(row_y + i, 4)).start()
+    def a_copy(source, target):
+        return remote(
+            flat,
+            abuf.at[rows16(source), :],
+            a_send.at[target],
+            a_recv.at[source],
+            (z, c, target * 4 + row_y),
+        )
+
+    @pl.loop(1, 4)
+    def _(i):
+        a_copy(row_x, lax.rem(row_x + i, 4)).start()
+
+    abuf[rows16(row_x), :] = flat[...]
 
     @after.append
     def _():
         @pl.loop(1, 4)
         def _(i):
-            a_copy(0, row_x, lax.rem(row_x + i, 4)).wait_send()
-            a_copy(1, row_y, lax.rem(row_y + i, 4)).wait_send()
-
-    abuf[row_x, row_y] = flat[...]
+            a_copy(row_x, lax.rem(row_x + i, 4)).wait_send()
 
     @pl.loop(1, DEPTH)
     def _(i):
         m_copy(lax.rem(z + i, DEPTH), z).wait_recv()
-
-    @pl.loop(1, 4)
-    def _(i):
-        a_copy(0, lax.rem(row_x + i, 4), row_x).wait_recv()
-
-    @pl.loop(1, 4)
-    def _(i):
-        b_copy(0, row_y, lax.rem(row_y + i, 4)).start()
-
-    @pl.loop(1, 4)
-    def _(i):
-        a_copy(1, lax.rem(row_y + i, 4), row_y).wait_recv()
-
-    @pl.loop(1, 4)
-    def _(i):
-        b_copy(1, row_x, lax.rem(row_x + i, 4)).start()
-
-    @after.append
-    def _():
-        @pl.loop(1, 4)
-        def _(i):
-            b_copy(0, row_y, lax.rem(row_y + i, 4)).wait_send()
-            b_copy(1, row_x, lax.rem(row_x + i, 4)).wait_send()
 
     meta = jnp.sum(mbuf[...], axis=0)
     expert_iota = lax.broadcasted_iota(jnp.int32, (16, 128), 0).astype(F32)
@@ -491,64 +504,68 @@
     turned_high = turned.astype(BF)
     turned_low = (turned - turned_high.astype(F32)).astype(BF)
 
-    w_copy(0).wait()
-
-    @pl.loop(1, 4)
-    def _(i):
-        b_copy(0, lax.rem(row_y + i, 4), row_y).wait_recv()
-        b_copy(1, lax.rem(row_x + i, 4), row_x).wait_recv()
-
-    projected = jnp.dot(abuf[...].reshape(256, 2048), w_ref[...], preferred_element_type=F32)
-    pstage[...] = projected.reshape(16, 16, 128)
-    own_side = lax.div(me, 8)
+    @pl.loop(1, 4)
+    def _(i):
+        k_copy(z + 1, lax.rem(row_y + i, 4), 0).wait_recv()
+        k_copy(z + 1, lax.rem(row_y + i, 4), 1).wait_recv()
+
+    @pl.loop(1, 4)
+    def _(i):
+        a_copy(lax.rem(row_x + i, 4), row_x).wait_recv()
+
+    gathered = abuf[...]
+    for part in range(4):
+        columns = jnp.dot(gathered, w_ref[part], preferred_element_type=F32)
+        pstage[:, :, part * 128 : part * 128 + 128] = columns.reshape(4, 16, 128)
+    own_side = lax.div(row_x, 2)
 
     def p_copy(source_core, source, target):
         return remote(
             pstage.at[target],
-            pbuf.at[source_core, lax.rem(source, 8)],
+            pbuf.at[source_core, lax.rem(source, 2)],
             p_send.at[target],
-            p_recv.at[source_core, lax.rem(source, 8)],
-            (z, lax.div(source, 8), target),
-        )
-
-    @pl.loop(1, PLANE)
-    def _(i):
-        p_copy(c, me, partner(i)).start()
+            p_recv.at[source_core, lax.rem(source, 2)],
+            (z, lax.div(source, 2), target * 4 + row_y),
+        )
+
+    @pl.loop(1, 4)
+    def _(i):
+        p_copy(c, row_x, lax.rem(row_x + i, 4)).start()
 
     @pl.when(own_side != c)
     def _():
-        p_copy(c, me, me).start()
-
-    @after.append
-    def _():
-        @pl.loop(1, PLANE)
-        def _(i):
-            p_copy(c, me, lax.rem(me + i, PLANE)).wait_send()
-
-    @after.append
-    def _():
+        p_copy(c, row_x, row_x).start()
+
+    @pl.when(own_side == c)
+    def _():
+        pbuf[c, lax.rem(row_x, 2)] = pstage[row_x]
+
+    @after.append
+    def _():
+        @pl.loop(1, 4)
+        def _(i):
+            p_copy(c, row_x, lax.rem(row_x + i, 4)).wait_send()
+
         @pl.when(own_side != c)
         def _():
-            p_copy(c, me, me).wait_send()
-
-    @pl.when(own_side == c)
-    def _():
-        pbuf[c, lax.rem(me, 8)] = pstage[me]
-
-    @pl.loop(0, 8)
-    def _(i):
-        p_copy(other, c * 8 + i, me).wait_recv()
-
-        @pl.when(c * 8 + i != me)
+            p_copy(c, row_x, row_x).wait_send()
+
+    @pl.loop(0, 2)
+    def _(i):
+        p_copy(other, c * 2 + i, row_x).wait_recv()
+
+        @pl.when(c * 2 + i != row_x)
         def _():
-            p_copy(c, c * 8 + i, me).wait_recv()
+            p_copy(c, c * 2 + i, row_x).wait_recv()
 
     mine = pl.ds(pl.multiple_of(c * 1024, 1024), 1024)
     theirs = pl.ds(pl.multiple_of(other * 1024, 1024), 1024)
     square = jnp.zeros((16, 128), F32)
     for part in range(8):
         cols = pl.ds(pl.multiple_of(c * 1024 + part * 128, 128), 128)
-        hidden = res_ref[:, cols].astype(F32) + (pbuf[0, part] + pbuf[1, part])
+        inner = slice(part % 4 * 128, part % 4 * 128 + 128)
+        arrived = pbuf[0, part // 4, :, inner] + pbuf[1, part // 4, :, inner]
+        hidden = res_ref[:, cols].astype(F32) + arrived
         hid_ref[:, part * 128 : part * 128 + 128] = hidden
         square = square + hidden * hidden
     sq_stage[...] = square
@@ -757,10 +774,10 @@
             pltpu.VMEM((PLANE, 272, 128), BF),
             pltpu.VMEM((16, 16, 128), F32),
             pltpu.VMEM((16, 2048), BF),
-            pltpu.VMEM((4, 4, 16, 2048), BF),
-            pltpu.VMEM((2048, 128), BF),
-            pltpu.VMEM((16, 16, 128), F32),
-            pltpu.VMEM((2, 8, 16, 128), F32),
+            pltpu.VMEM((64, 2048), BF),
+            pltpu.VMEM((4, 2048, 128), BF),
+            pltpu.VMEM((4, 16, 512), F32),
+            pltpu.VMEM((2, 2, 16, 512), F32),
             pltpu.VMEM((16, 1024), F32),
             pltpu.VMEM((16, 128), F32),
             pltpu.VMEM((16, 128), F32),
@@ -788,12 +805,14 @@
             dma(2, 4),
             dma(PLANE),
             dma(PLANE),
+            dma(4),
+            dma(4),
             dma(2, 4),
             dma(2, 4),
             dma(2, 4),
             dma(2, 4),
-            dma(PLANE),
-            dma(2, 8),
+            dma(4),
+            dma(2, 2),
             dma(2),
             dma(DEPTH),
             dma(DEPTH),

time: 107 us -> 105 us (0.981)
  Pallas kernels: 105 us -> 103 us
    pallas_call x1, Pallas kernels: 105 us -> 103 us  [layer(): pl.pallas_call(functools.partial(layer_kernel, span), out_shape=jax.Shape...]
where the time goes in v4:
time: 105 us; the launch traced here: 104 us
  Pallas kernels  103 us (98%)
  local copies, waits for them, and re-layouts  1.38 us (1%)
    pallas_call x1, Pallas kernels, layer(): pl.pallas_call(functools.partial(layer_kernel, span), out_shape=jax.Shape...  103 us

profile of v4, /device:TPU:1, one launch (start us, length us, event | category | flops | bytes accessed | tf_op | source)
XLA Modules:
  0.0 104.3 jit_solution(14796873982284312611)
XLA Ops:
  0.0 102.9 %shard_map.127 = bf16[16,1024]{1,0:T(8,128)(2,1)} custom-call(bf16[4,64,128]{2,1,0:T(8,128)(2,1)} %bitcast.14, bf16[4,8,128]{2,1,0:T(8,128)(2,1)} %bitcast.15, bf16[4,8,128]{2,1,0:T(8,128)(2,1)} %bitcast.16, bf16[4,3072,128]{2,1,0:T(8,128)(2,1)} %bitcast.10, bf16[4,3072,128]{2,1,0:T(8,128)(2,1)} %bitcast.11, s32[4]{0:T(128)} %len_ref.1, ...), custom_call_target="tpu_custom_call" | custom-call | tf_op jit(solution)/shard_map/pallas_call | solution.py:757
  103.0 1.4 %copy.15 = bf16[16,1024]{1,0:T(8,128)(2,1)} copy(bf16[16,1024]{1,0:T(8,128)(2,1)} %shard_map.127) | data formatting | bytes 65536

commit v5 on v4

--- a/solution.py
+++ b/solution.py
@@ -130,6 +130,12 @@
     row_x = lax.div(me, 4)
     row_y = lax.rem(me, 4)
 
+    def far_first(i):
+        near = DEPTH - i
+        half = lax.div(near + 1, 2)
+        odd = lax.rem(near, 2)
+        return odd * half + (1 - odd) * (DEPTH - half)
+
     sign = 1 - 2 * lax.rem(row_x + row_y, 2)
 
     def moved(way, step_x, step_y):
@@ -271,31 +277,6 @@
             target[request, tail, 0:128] = loose[pl.ds(0, 128, 2), :].astype(BF)
             target[request, tail, 128:256] = loose[pl.ds(1, 128, 2), :].astype(BF)
 
-    arrange(2)
-
-    @pl.loop(1, 4)
-    def _(i):
-        q_copy(1, lax.rem(row_y + i, 4), row_y).wait_recv()
-
-    @pl.loop(1, 4)
-    def _(i):
-        f_copy(1, row_x, lax.rem(row_x + i, 4)).start()
-
-    @pl.loop(1, 4)
-    def _(i):
-        q_copy(0, lax.rem(row_x + i, 4), row_x).wait_recv()
-
-    @pl.loop(1, 4)
-    def _(i):
-        f_copy(0, row_y, lax.rem(row_y + i, 4)).start()
-
-    @after.append
-    def _():
-        @pl.loop(1, 4)
-        def _(i):
-            f_copy(0, row_y, lax.rem(row_y + i, 4)).wait_send()
-            f_copy(1, row_x, lax.rem(row_x + i, 4)).wait_send()
-
     def w_rows(side, batch):
         return pl.ds(pl.multiple_of(lax.rem(side, 2) * 1024 + batch * 512, 512), 512)
 
@@ -325,6 +306,31 @@
         @pl.loop(1, 4)
         def _(i):
             g_copy(row_y, lax.rem(row_y + i, 4), batch).start()
+
+    arrange(2)
+
+    @pl.loop(1, 4)
+    def _(i):
+        q_copy(1, lax.rem(row_y + i, 4), row_y).wait_recv()
+
+    @pl.loop(1, 4)
+    def _(i):
+        f_copy(1, row_x, lax.rem(row_x + i, 4)).start()
+
+    @pl.loop(1, 4)
+    def _(i):
+        q_copy(0, lax.rem(row_x + i, 4), row_x).wait_recv()
+
+    @pl.loop(1, 4)
+    def _(i):
+        f_copy(0, row_y, lax.rem(row_y + i, 4)).start()
+
+    @after.append
+    def _():
+        @pl.loop(1, 4)
+        def _(i):
+            f_copy(0, row_y, lax.rem(row_y + i, 4)).wait_send()
+            f_copy(1, row_x, lax.rem(row_x + i, 4)).wait_send()
 
     @after.append
     def _():
@@ -585,7 +591,7 @@
 
     @pl.loop(1, DEPTH)
     def _(i):
-        z_copy(z, lax.rem(z + i, DEPTH)).start()
+        z_copy(z, lax.rem(z + far_first(i), DEPTH)).start()
 
     @after.append
     def _():
@@ -721,7 +727,7 @@
 
     @pl.loop(1, DEPTH)
     def _(i):
-        c_copy(z, lax.rem(z + i, DEPTH)).start()
+        c_copy(z, lax.rem(z + far_first(i), DEPTH)).start()
 
     @after.append
     def _():

time: 105 us -> 106 us (level)
    pallas_call x1, Pallas kernels: 103 us -> 104 us  [layer(): pl.pallas_call(functools.partial(layer_kernel, span), out_shape=jax.Shape...]
where the time goes in v5:
time: 106 us
  Pallas kernels  104 us (98%)
  local copies, waits for them, and re-layouts  1.38 us (1%)
    pallas_call x1, Pallas kernels, layer(): pl.pallas_call(functools.partial(layer_kernel, span), out_shape=jax.Shape...  104 us

profile of v5, /device:TPU:1, one launch (start us, length us, event | category | flops | bytes accessed | tf_op | source)
XLA Modules:
  0.0 105.8 jit_solution(8999292943594348103)
XLA Ops:
  0.0 104.5 %shard_map.127 = bf16[16,1024]{1,0:T(8,128)(2,1)} custom-call(bf16[4,64,128]{2,1,0:T(8,128)(2,1)} %bitcast.14, bf16[4,8,128]{2,1,0:T(8,128)(2,1)} %bitcast.15, bf16[4,8,128]{2,1,0:T(8,128)(2,1)} %bitcast.16, bf16[4,3072,128]{2,1,0:T(8,128)(2,1)} %bitcast.10, bf16[4,3072,128]{2,1,0:T(8,128)(2,1)} %bitcast.11, s32[4]{0:T(128)} %len_ref.1, ...), custom_call_target="tpu_custom_call" | custom-call | tf_op jit(solution)/shard_map/pallas_call | solution.py:763
  104.5 1.4 %copy.15 = bf16[16,1024]{1,0:T(8,128)(2,1)} copy(bf16[16,1024]{1,0:T(8,128)(2,1)} %shard_map.127) | data formatting | bytes 65536
